TPU v7x, 512 devices: a whole 4x4x16 slice. The times are simulated.
512 devices in a mesh: row: 64 (over y, z), col: 8 (over x, core).
Axes of the slice: x: 4, y: 4, z: 16, core: 2. Of those that a mesh axis runs over, the one named last changes fastest.
Arguments:
- embeddings: bfloat16 [65536, 16384], P('row', 'col'), may hold values from -0.046875 to 0.046875
- targets: float32 [65536, 16], P('row'), may hold values from -64 to 64
- classes: int32 [65536], P('row'), may hold values 0 or 1
- start_coef: float32 [16384, 16], P('col'), may hold values from -6 to 6
Outputs:
- coef_next: float32 [16384, 16], P('col')
- resid_next: float32 [65536, 16], P('row')
- direction_next: float32 [16384, 16], P('col')
All inputs are finite; a program needn't handle non-finite values. No bound on the sum of `classes` on one device may be relied on, other than what follows from the above.
Results may differ from a plain program's by a relative error of at most 0.0086.
Values sent between devices are 32-bit elements; how exact they have to be, the bound alone decides.
A program may use at most 64 MiB of HBM per device.

v0:
```python
import jax
import jax.numpy as jnp
from jax import lax
from jax.sharding import PartitionSpec as P

huber_delta = 8.0


def transposed(left, right):
    return lax.dot_general(
        left, right, (((0,), (0,)), ((), ())), preferred_element_type=jnp.float32
    )


def shards(embeddings, targets, classes, start_coef):
    rows_here, cols_here = embeddings.shape
    all_rows = rows_here * lax.axis_size("row")
    pred_part = jnp.dot(
        embeddings, start_coef.astype(jnp.bfloat16), preferred_element_type=jnp.float32
    )
    predicted = lax.psum(pred_part, "col")
    resid_start = targets - predicted
    res_norm = jnp.sqrt(jnp.sum(resid_start * resid_start, axis=1))
    raw_weight = jnp.where(
        classes == 1, huber_delta / jnp.maximum(huber_delta, res_norm), jnp.float32(1.0)
    )
    weighted = (raw_weight[:, None] * resid_start).astype(jnp.bfloat16)
    grad_raw = lax.psum(transposed(embeddings, weighted), "row")
    gamma_raw = lax.psum(jnp.sum(grad_raw * grad_raw, axis=0), "col")
    image_part = jnp.dot(
        embeddings, grad_raw.astype(jnp.bfloat16), preferred_element_type=jnp.float32
    )
    image_raw = lax.psum(image_part, "col")
    curv_part = jnp.sum(raw_weight[:, None] * image_raw * image_raw, axis=0)
    weight_sum = jnp.sum(raw_weight)
    total = lax.psum(weight_sum, "row")
    curv_raw = lax.psum(curv_part, "row")
    mean_weight = total / all_rows
    gamma = gamma_raw / (mean_weight * mean_weight)
    curvature = curv_raw / (mean_weight * mean_weight * mean_weight)
    alpha = gamma / curvature
    coef_next = start_coef + alpha * (grad_raw / mean_weight)
    resid_next = resid_start - alpha * (image_raw / mean_weight)
    weighted_next = (raw_weight[:, None] * resid_next).astype(jnp.bfloat16)
    grad_next = lax.psum(transposed(embeddings, weighted_next), "row")
    square_next = lax.psum(jnp.sum(grad_next * grad_next, axis=0), "col")
    beta = square_next / (mean_weight * mean_weight) / gamma
    direction_next = grad_next / mean_weight + beta * (grad_raw / mean_weight)
    return (coef_next, resid_next, direction_next)


def solution(mesh):
    return jax.shard_map(
        shards,
        mesh=mesh,
        in_specs=(P("row", "col"), P("row", None), P("row"), P("col", None)),
        out_specs=(P("col", None), P("row", None), P("col", None)),
        check_vma=False,
    )
```

profile of v0, /device:TPU:1, one launch (start us, length us, event | category | flops | bytes accessed | tf_op | source)
XLA Modules:
  0.0 850.1 jit_solution(6218840132495395205)
XLA Ops:
  7.2 0.0 all-reduce.6.cloned.1.call-start
  7.2 4.0 fusion.2
  11.3 0.0 all-reduce.6.cloned.1.call-update
  11.3 0.0 all-reduce.8.cloned.1.call-start
  11.3 78.1 %all-reduce.6.cloned.1.call-done = f32[1024,16]{0,1:T(8,128)} async-done(((f32[1024,16]{0,1:T(8,128)}), f32[1024,16]{0,1:T(8,128)}) %all-reduce.6.cloned.1.call-update) | async-done | bytes 65552 | tf_op jit(solution)/shard_map/psum | solution.py:21
  89.5 0.9 multiply_reduce_fusion.2
  90.3 0.6 fusion.6
  90.9 3.5 convolution_bitcast_fusion.1
  94.4 0.0 all-reduce.8.cloned.1.call-update
  94.5 0.0 all-reduce.10.cloned.1.call-start
  94.5 250.8 %all-reduce.8.cloned.1.call-done = f32[2048,16]{0,1:T(8,128)} async-done(((f32[2048,16]{0,1:T(8,128)}), f32[2048,16]{0,1:T(8,128)}) %all-reduce.8.cloned.1.call-update) | async-done | bytes 131088 | tf_op jit(solution)/shard_map/psum | solution.py:28
  345.4 4.1 convolution_bitcast_fusion.2
  349.5 0.0 all-reduce.12.cloned.1.call-start
  349.6 0.1 multiply_reduce_fusion.1
  349.7 22.9 %psum.58 = f32[16]{0:T(128)S(1)} all-reduce(f32[16]{0:T(128)S(1)} %multiply_reduce_fusion.1), channel_id=1, replica_groups=mesh['row'=64,'col'=8] {'col'}, use_global_device_ids=true, to_apply=%region_4.5 | all-reduce | flops 16 | bytes 128 | tf_op jit(solution)/shard_map/psum | solution.py:29
  372.6 54.6 %all-reduce.10.cloned.1.call-done = f32[1024,16]{0,1:T(8,128)} async-done(((f32[1024,16]{0,1:T(8,128)}), f32[1024,16]{0,1:T(8,128)}) %all-reduce.10.cloned.1.call-update) | async-done | bytes 65552 | tf_op jit(solution)/shard_map/psum | solution.py:33
  427.2 1.0 fusion
  428.1 116.5 %all-reduce = (f32[16]{0:T(128)S(1)}, f32[]{:T(128)}) all-reduce(f32[16]{0:T(128)S(1)} %fusion, f32[]{:T(128)} %get-tuple-element.5), channel_id=1, replica_groups=mesh['row'=64,'col'=8] {'row'}, use_global_device_ids=true, to_apply=%region_9.10 | all-reduce | flops 17 | bytes 136 | tf_op jit(solution)/shard_map/psum | solution.py:37
  547.3 0.9 multiply_subtract_fusion
  548.2 3.5 convolution_bitcast_fusion
  551.7 266.2 %all-reduce.12.cloned.1.call-done = f32[2048,16]{0,1:T(8,128)} async-done(((f32[2048,16]{0,1:T(8,128)}), f32[2048,16]{0,1:T(8,128)}) %all-reduce.12.cloned.1.call-update) | async-done | bytes 131088 | tf_op jit(solution)/shard_map/psum | solution.py:45
  817.9 1.0 multiply_reduce_fusion
  818.9 22.9 %psum.63 = f32[16]{0:T(128)S(1)} all-reduce(f32[16]{0:T(128)S(1)} %multiply_reduce_fusion), channel_id=1, replica_groups=mesh['row'=64,'col'=8] {'col'}, use_global_device_ids=true, to_apply=%region_12.13 | all-reduce | flops 16 | bytes 128 | tf_op jit(solution)/shard_map/psum | solution.py:46
  841.9 1.7 multiply_add_fusion
  (14 shorter events, 0.1 us)
Async XLA Ops:
  7.2 82.3 %copy-start.3 = (f32[1024,16]{0,1:T(8,128)S(1)}, f32[1024,16]{0,1:T(8,128)}, u32[]{:S(2)}) copy-start(f32[1024,16]{0,1:T(8,128)} %param.5) | copy-start | bytes 196612
  7.2 83.1 %copy-start.4 = (s32[1024]{0:T(1024)S(1)}, s32[1024]{0:T(1024)}, u32[]{:S(2)}) copy-start(s32[1024]{0:T(1024)} %param.6) | copy-start | bytes 12292
  7.2 82.3 %all-reduce.6.cloned.1.call-start = ((), (), s32[]{:S(2)}) async-start(), calls=%async_computation | async-start | bytes 131072 | tf_op jit(solution)/shard_map/psum | solution.py:21
  11.3 334.1 %all-reduce.8.cloned.1.call-start = ((), (), s32[]{:S(2)}) async-start(), calls=%async_computation.1 | async-start | bytes 262144 | tf_op jit(solution)/shard_map/psum | solution.py:28
  94.5 747.4 %copy-start.1 = (f32[2048,16]{0,1:T(8,128)S(1)}, f32[2048,16]{0,1:T(8,128)}, u32[]{:S(2)}) copy-start(f32[2048,16]{0,1:T(8,128)} %param.7) | copy-start | bytes 393220
  94.5 332.7 %all-reduce.10.cloned.1.call-start = ((), (), s32[]{:S(2)}) async-start(), calls=%async_computation.2 | async-start | bytes 131072 | tf_op jit(solution)/shard_map/psum | solution.py:33
  345.4 4.2 copy-start
  349.5 468.4 %all-reduce.12.cloned.1.call-start = ((), (), s32[]{:S(2)}) async-start(), calls=%async_computation.3 | async-start | bytes 262144 | tf_op jit(solution)/shard_map/psum | solution.py:45
  548.2 295.4 %copy-start.2 = (f32[1024,16]{0,1:T(8,128)}, f32[1024,16]{0,1:T(8,128)S(1)}, u32[]{:S(2)}) copy-start(f32[1024,16]{0,1:T(8,128)S(1)} %multiply_subtract_fusion) | copy-start | bytes 196612
Sparse Core Ops, SparseCore 0:
  11.4 78.0 all-reduce.5
  94.6 250.7 all-reduce.7
  349.6 77.4 all-reduce.9
  551.9 266.0 all-reduce.11
where the time goes:
time: 851 us; the launch traced here: 850 us
  waiting for transfers between devices  650 us (76%)
  blocking collectives  162 us (19%)
  between operations  16.4 us (2%)
  matrix products  15.2 us (2%)
    psum x1, waiting for transfers between devices, shards(): grad_next = lax.psum(transposed(embeddings, weighted_next), 'row')  266 us
    psum x1, waiting for transfers between devices, shards(): grad_raw = lax.psum(transposed(embeddings, weighted), 'row')  251 us
    psum x1, blocking collectives, shards(): curv_raw = lax.psum(curv_part, 'row')  117 us
    psum x1, waiting for transfers between devices, shards(): predicted = lax.psum(pred_part, 'col')  78.1 us
    psum x1, waiting for transfers between devices, shards(): image_raw = lax.psum(image_part, 'col')  54.6 us
    psum x1, blocking collectives, shards(): gamma_raw = lax.psum(jnp.sum(grad_raw * grad_raw, axis=0), 'col')  22.9 us
    psum x1, blocking collectives, shards(): square_next = lax.psum(jnp.sum(grad_next * grad_next, axis=0), 'col')  22.9 us
  transfers between devices with their start and end apart: 4, of which 4 were waited for; matrix products, arithmetic and copies ran while one was open for 0% of the time, Pallas kernels for 0%

commit v1 on v0

v1 whole, which is shorter than its diff:
```python
import functools

import jax
import jax.numpy as jnp
from jax import lax
from jax.experimental import pallas as pl
from jax.experimental.pallas import tpu as pltpu
from jax.sharding import PartitionSpec as P

MESH = pl.DeviceIdType.MESH
huber_delta = 8.0
LANES = 128
PIECE = 4
Y_CHIPS = 4

BF16 = jnp.bfloat16
F32 = jnp.float32

(X1_RS, X1_AG, Y1_RS, Z1_RS, Z1_AG, Y1_AG, GAMMA, X2_RS, X2_AG,
 SCAL_Y, SCAL_Z, Y2_RS, Z2_RS, Z2_AG, Y2_AG, SQUARE) = range(16)


def drain(ref, sem):
    pltpu.make_async_copy(ref, ref, sem).wait()


def kernel(ny, nz, nc, resp, all_rows,
           e_hbm, t_hbm, cls_hbm, c_hbm,
           coef_out, resid_out, dir_out,
           e, t, cls, coef, cb, w, resid, lhs, g, gn,
           part, xrecv, xfull, yrecv, ypart, ysum, zrecv, gath,
           row_x, row_y, row_z, row_mine,
           load_sem, send_sem, recv_sem):
    rows_here, feats = e.shape
    quarter = feats // ny
    tiles = quarter // LANES
    per_tile = resp // PIECE
    here = lax.axis_index("row")
    col = lax.axis_index("col")
    y, z = lax.div(here, nz), lax.rem(here, nz)

    def x_peer(step):
        return here, lax.rem(col + step, nc)

    def y_peer(step):
        other = lax.rem(y + step, ny)
        return other * nz + z, col

    def z_peer(step):
        other = lax.rem(z + step, nz)
        return y * nz + other, col

    def far_first(k, n):
        return n // 2 + lax.div(k + 1, 2) * (2 * lax.rem(k, 2) - 1)

    def each(n, body):
        def step(k, _):
            body(far_first(k, n))
            return 0

        lax.fori_loop(0, n - 1, step, 0)

    def send(which, src, dst, peer):
        pltpu.make_async_remote_copy(
            src_ref=src, dst_ref=dst,
            send_sem=send_sem.at[which], recv_sem=recv_sem.at[which],
            device_id=peer, device_id_type=MESH,
        ).start()

    load_c = pltpu.make_async_copy(c_hbm, coef, load_sem.at[0])
    load_t = pltpu.make_async_copy(t_hbm, t, load_sem.at[1])
    load_cls = pltpu.make_async_copy(cls_hbm, cls, load_sem.at[2])
    load_c.start()

    def chunk(step):
        j = lax.rem(col + 1 + step, nc)
        rows = pl.ds(pl.multiple_of(j * LANES, LANES), LANES)
        return j, rows, pltpu.make_async_copy(
            e_hbm.at[rows], e.at[rows], load_sem.at[3 + step])

    for step in range(nc):
        chunk(step)[2].start()
    load_t.start()
    load_cls.start()

    barrier = pltpu.get_barrier_semaphore()

    def greet(peer_of):
        def inner(step):
            pl.semaphore_signal(barrier, inc=1, device_id=peer_of(step), device_id_type=MESH)
        return inner

    each(nc, greet(x_peer))
    each(ny, greet(y_peer))
    each(nz, greet(z_peer))

    def times_rows(left, rows):
        return lax.dot_general(
            left, e[rows, :], (((1,), (1,)), ((), ())), preferred_element_type=F32)

    def x_reduce(which_rs, which_ag, buf, after_first, loading, left):
        def product(step):
            j, rows, load = chunk(step)
            if loading:
                load.wait()
            part[buf, j] = times_rows(left[...], rows)
            return j

        first = product(0)
        after_first()
        send(which_rs, part.at[buf, first], xrecv.at[buf, col], (here, first))

        def more(step, _):
            j = product(step)
            send(which_rs, part.at[buf, j], xrecv.at[buf, col], (here, j))
            return 0

        lax.fori_loop(1, nc - 1, more, 0)
        product(nc - 1)
        xrecv[buf, col] = part[buf, col]
        drain(xrecv.at[buf, pl.ds(0, nc - 1)], recv_sem.at[which_rs])
        xfull[buf, col] = jnp.sum(xrecv[buf], axis=0)
        each(nc, lambda step: send(
            which_ag, xfull.at[buf, col], xfull.at[buf, col], x_peer(step)))
        drain(xfull.at[buf, pl.ds(0, nc - 1)], recv_sem.at[which_ag])

    def y_reduce(which, buf):
        def product(other):
            lanes = pl.ds(pl.multiple_of(other * quarter, quarter), quarter)
            both = jnp.dot(lhs[...], e[:, lanes], preferred_element_type=F32)
            total = both[:resp] + both[resp:]
            for tile in range(tiles):
                for q in range(per_tile):
                    ypart[buf, other, tile * per_tile + q] = total[
                        q * PIECE:(q + 1) * PIECE, tile * LANES:(tile + 1) * LANES]

        def more(k, _):
            other = lax.rem(y + far_first(k, ny), ny)
            product(other)
            send(which, ypart.at[buf, other], yrecv.at[buf, y], (other * nz + z, col))
            return 0

        lax.fori_loop(0, ny - 1, more, 0)
        product(y)
        yrecv[buf, y] = ypart[buf, y]

    def z_reduce(which_y, which_z, buf):
        drain(yrecv.at[buf, pl.ds(0, ny - 1)], recv_sem.at[which_y])
        ysum[buf] = jnp.sum(yrecv[buf], axis=0)
        each(nz, lambda step: send(
            which_z, ysum.at[buf, lax.rem(z + step, nz)], zrecv.at[buf, z], z_peer(step)))
        zrecv[buf, z] = ysum[buf, z]

    def z_gather(which_rs, which_ag, buf):
        drain(zrecv.at[buf, pl.ds(0, nz - 1)], recv_sem.at[which_rs])
        gath[buf, y, z] = jnp.sum(zrecv[buf], axis=0)
        each(nz, lambda step: send(
            which_ag, gath.at[buf, y, z], gath.at[buf, y, z], z_peer(step)))

    def y_gather(which_z, which_y, buf):
        drain(gath.at[buf, 0, pl.ds(0, nz - 1)], recv_sem.at[which_z])
        each(ny, lambda step: send(which_y, gath.at[buf, y], gath.at[buf, y], y_peer(step)))
        drain(gath.at[buf, pl.ds(0, ny - 1)], recv_sem.at[which_y])

    def assembled(buf, other, tile):
        return jnp.concatenate(
            [gath[buf, other, tile * per_tile + q] for q in range(per_tile)], axis=0)

    lane = lax.broadcasted_iota(jnp.int32, (resp, LANES), 1)
    sub = lax.broadcasted_iota(jnp.int32, (resp, LANES), 0)
    diagonal = lane == sub

    def to_row(column):
        return jnp.sum(jnp.where(diagonal, column, 0.0), axis=0, keepdims=True)

    def to_column(row):
        return jnp.sum(jnp.where(diagonal, row, 0.0), axis=1, keepdims=True)

    load_c.wait()
    cb[...] = coef[...].astype(BF16)
    x_reduce(X1_RS, X1_AG, 0,
             lambda: pl.semaphore_wait(barrier, (nc - 1) + (ny - 1) + (nz - 1)),
             True, cb)
    load_t.wait()
    load_cls.wait()

    def put_pair(j, value):
        high = value.astype(BF16)
        low = (value - high.astype(F32)).astype(BF16)
        lanes = slice(j * LANES, (j + 1) * LANES)
        lhs[0:resp, lanes] = high
        lhs[resp:2 * resp, lanes] = low

    for j in range(nc):
        r = t[:, j * LANES:(j + 1) * LANES] - xfull[0, j]
        resid[j] = r
        norm = jnp.sqrt(jnp.sum(r * r, axis=0, keepdims=True))
        weight = jnp.where(
            cls[j:j + 1, :] == 1, huber_delta / jnp.maximum(huber_delta, norm), 1.0)
        w[j:j + 1, :] = weight
        put_pair(j, weight * r)

    y_reduce(Y1_RS, 0)
    z_reduce(Y1_RS, Z1_RS, 0)
    z_gather(Z1_RS, Z1_AG, 0)
    y_gather(Z1_AG, Y1_AG, 0)
    norm2 = jnp.zeros((resp, LANES), F32)
    for other in range(ny):
        for tile in range(tiles):
            piece = assembled(0, other, tile)
            lanes = slice(other * quarter + tile * LANES, other * quarter + (tile + 1) * LANES)
            g[:, lanes] = piece
            cb[:, lanes] = piece.astype(BF16)
            norm2 = norm2 + piece * piece
    row_x[0, col] = to_row(jnp.sum(norm2, axis=1, keepdims=True))
    each(nc, lambda step: send(GAMMA, row_x.at[0, col], row_x.at[0, col], x_peer(step)))

    x_reduce(X2_RS, X2_AG, 1, lambda: None, False, cb)
    curv = jnp.zeros((resp, LANES), F32)
    weight_sum = jnp.zeros((1, LANES), F32)
    for j in range(nc):
        weight = w[j:j + 1, :]
        image = xfull[1, j]
        scaled = weight * image
        curv = curv + scaled * image
        weight_sum = weight_sum + weight
        put_pair(j, scaled)
    mine = to_row(jnp.sum(curv, axis=1, keepdims=True)) + jnp.where(
        lane[0:1] == resp, jnp.sum(weight_sum, axis=1, keepdims=True), 0.0)
    row_y[y] = mine
    each(ny, lambda step: send(SCAL_Y, row_y.at[y], row_y.at[y], y_peer(step)))

    y_reduce(Y2_RS, 1)
    drain(row_y.at[pl.ds(0, ny - 1)], recv_sem.at[SCAL_Y])
    row_z[z] = jnp.sum(row_y[...], axis=0)
    each(nz, lambda step: send(SCAL_Z, row_z.at[z], row_z.at[z], z_peer(step)))
    z_reduce(Y2_RS, Z2_RS, 1)

    drain(row_x.at[0, pl.ds(0, nc - 1)], recv_sem.at[GAMMA])
    drain(row_z.at[pl.ds(0, nz - 1)], recv_sem.at[SCAL_Z])
    sums = jnp.sum(row_z[...], axis=0)
    gamma_raw = to_column(jnp.sum(row_x[0], axis=0))
    curv_raw = to_column(sums)
    mean = jnp.sum(jnp.where(lane[0:1] == resp, sums, 0.0), axis=1, keepdims=True) / all_rows
    gamma = gamma_raw / (mean * mean)
    alpha = gamma / (curv_raw / (mean * mean * mean))
    z_gather(Z2_RS, Z2_AG, 1)
    coef_out[...] = coef[...] + alpha * (g[...] / mean)
    for j in range(nc):
        resid_out[:, j * LANES:(j + 1) * LANES] = resid[j] - alpha * (xfull[1, j] / mean)
    y_gather(Z2_AG, Y2_AG, 1)

    ratio = alpha / mean
    norm2 = jnp.zeros((resp, LANES), F32)
    for other in range(ny):
        for tile in range(tiles):
            lanes = slice(other * quarter + tile * LANES, other * quarter + (tile + 1) * LANES)
            piece = g[:, lanes] - ratio * assembled(1, other, tile)
            gn[:, lanes] = piece
            norm2 = norm2 + piece * piece
    row_x[1, col] = to_row(jnp.sum(norm2, axis=1, keepdims=True))
    each(nc, lambda step: send(SQUARE, row_x.at[1, col], row_x.at[1, col], x_peer(step)))
    drain(row_x.at[1, pl.ds(0, nc - 1)], recv_sem.at[SQUARE])
    square = to_column(jnp.sum(row_x[1], axis=0))
    beta = square / (mean * mean) / gamma
    dir_out[...] = gn[...] / mean + beta * (g[...] / mean)

    for which, ref in (
        (X1_RS, xrecv.at[0, pl.ds(0, nc - 1)]), (X2_RS, xrecv.at[1, pl.ds(0, nc - 1)]),
        (X1_AG, xfull.at[0, pl.ds(0, nc - 1)]), (X2_AG, xfull.at[1, pl.ds(0, nc - 1)]),
        (Y1_RS, yrecv.at[0, pl.ds(0, ny - 1)]), (Y2_RS, yrecv.at[1, pl.ds(0, ny - 1)]),
        (Z1_RS, zrecv.at[0, pl.ds(0, nz - 1)]), (Z2_RS, zrecv.at[1, pl.ds(0, nz - 1)]),
        (Z1_AG, zrecv.at[0, pl.ds(0, nz - 1)]), (Z2_AG, zrecv.at[1, pl.ds(0, nz - 1)]),
        (Y1_AG, gath.at[0, pl.ds(0, ny - 1)]), (Y2_AG, gath.at[1, pl.ds(0, ny - 1)]),
        (GAMMA, row_x.at[0, pl.ds(0, nc - 1)]), (SQUARE, row_x.at[1, pl.ds(0, nc - 1)]),
        (SCAL_Y, row_y.at[pl.ds(0, ny - 1)]), (SCAL_Z, row_z.at[pl.ds(0, nz - 1)]),
    ):
        drain(ref, send_sem.at[which])


def shards(ny, embeddings, targets, classes, start_coef):
    rows_here, feats = embeddings.shape
    resp = targets.shape[1]
    all_rows = rows_here * lax.axis_size("row")
    nc = lax.axis_size("col")
    nz = lax.axis_size("row") // ny
    vmem = pltpu.VMEM
    coef_next, resid_next, direction_next = pl.pallas_call(
        functools.partial(kernel, ny, nz, nc, resp, float(all_rows)),
        out_shape=(
            jax.ShapeDtypeStruct((resp, feats), F32),
            jax.ShapeDtypeStruct((resp, rows_here), F32),
            jax.ShapeDtypeStruct((resp, feats), F32),
        ),
        in_specs=[pl.BlockSpec(memory_space=pl.ANY)] * 4,
        out_specs=(pl.BlockSpec(memory_space=pltpu.VMEM),) * 3,
        scratch_shapes=[
            vmem((rows_here, feats), BF16),
            vmem((resp, rows_here), F32),
            vmem((nc, LANES), jnp.int32),
            vmem((resp, feats), F32),
            vmem((resp, feats), BF16),
            vmem((nc, LANES), F32),
            vmem((nc, resp, LANES), F32),
            vmem((2 * resp, rows_here), BF16),
            vmem((resp, feats), F32),
            vmem((resp, feats), F32),
            vmem((2, nc, resp, LANES), F32),
            vmem((2, nc, resp, LANES), F32),
            vmem((2, nc, resp, LANES), F32),
            vmem((2, ny, nz, PIECE, LANES), F32),
            vmem((2, ny, nz, PIECE, LANES), F32),
            vmem((2, nz, PIECE, LANES), F32),
            vmem((2, nz, PIECE, LANES), F32),
            vmem((2, ny, nz, PIECE, LANES), F32),
            vmem((2, nc, 1, LANES), F32),
            vmem((ny, 1, LANES), F32),
            vmem((nz, 1, LANES), F32),
            vmem((1, LANES), F32),
            pltpu.SemaphoreType.DMA((3 + nc,)),
            pltpu.SemaphoreType.DMA((16,)),
            pltpu.SemaphoreType.DMA((16,)),
        ],
        compiler_params=pltpu.CompilerParams(
            collective_id=0, has_side_effects=True, vmem_limit_bytes=32 * 1024 * 1024),
    )(embeddings, targets.T, classes.reshape(nc, LANES), start_coef.T)
    return coef_next.T, resid_next.T, direction_next.T


def solution(mesh, y_chips=Y_CHIPS):
    return jax.shard_map(
        functools.partial(shards, y_chips),
        mesh=mesh,
        in_specs=(P("row", "col"), P("row", None), P("row"), P("col", None)),
        out_specs=(P("col", None), P("row", None), P("col", None)),
        check_vma=False,
    )
```

time: 851 us -> 89.9 us (0.11)
  waiting for transfers between devices: 650 us -> 0 us
  blocking collectives: 162 us -> 0 us
  Pallas kernels: 0 us -> 82.4 us
  between operations: 16.4 us -> 0.65 us
  matrix products: 15.2 us -> 0 us
    psum x4 -> x0, waiting for transfers between devices: 650 us -> none  [the longest x1 266 us: shards(): grad_next = lax.psum(transposed(embeddings, weighted_next), 'row')]
    psum x3 -> x0, blocking collectives: 162 us -> none  [the longest x1 117 us: shards(): curv_raw = lax.psum(curv_part, 'row')]
    pallas_call x0 -> x1, Pallas kernels: none -> 82.4 us  [shards(): pl.pallas_call(functools.partial(kernel, ny, nz, nc, resp, float(all_rows...]
    dot_general x4 -> x0, matrix products: 15.2 us -> none  [the longest x2 7.03 us: transposed(): lax.dot_general(left, right, (((0,), (0,)), ((), ())), preferred_element_...]
  transfers between devices with their start and end apart: 4 -> 0, of which waited for: 4 -> 0; matrix products, arithmetic and copies ran while one was open for 0% -> 0% of each run, Pallas kernels for 0% -> 0%
where the time goes in v1:
time: 89.9 us; the launch traced here: 89.6 us
  Pallas kernels  82.4 us (92%)
  local copies, waits for them, and re-layouts  6.55 us (7%)
    pallas_call x1, Pallas kernels, shards(): pl.pallas_call(functools.partial(kernel, ny, nz, nc, resp, float(all_rows...  82.4 us
    unnamed x11, local copies, waits for them, and re-layouts  6.55 us

profile of v1, /device:TPU:1, one launch (start us, length us, event | category | flops | bytes accessed | tf_op | source)
XLA Modules:
  0.0 89.6 jit_solution(7788942890149360428)
XLA Ops:
  0.6 0.0 copy-start
  0.6 2.2 %copy-done = bf16[1024,2048]{1,0:T(8,128)(2,1)S(1)} copy-done((bf16[1024,2048]{1,0:T(8,128)(2,1)S(1)}, bf16[1024,2048]{1,0:T(8,128)(2,1)}, u32[]{:S(2)}) %copy-start) | copy-done | bytes 4194328
  2.8 0.0 copy-start.1
  2.8 0.9 %copy-done.1 = f32[2048,16]{0,1:T(8,128)S(1)} copy-done((f32[2048,16]{0,1:T(8,128)S(1)}, f32[2048,16]{0,1:T(8,128)}, u32[]{:S(2)}) %copy-start.1) | copy-done | bytes 131096
  3.7 0.0 copy-start.2
  3.7 0.8 copy-done.2
  4.6 0.0 copy-start.3
  4.6 0.7 copy-done.3
  5.3 82.4 %shard_map.67 = (f32[16,2048]{1,0:T(8,128)S(1)}, f32[16,1024]{1,0:T(8,128)S(1)}, f32[16,2048]{1,0:T(8,128)S(1)}) custom-call(bf16[1024,2048]{1,0:T(8,128)(2,1)S(1)} %copy-done, f32[16,1024]{1,0:T(8,128)S(1)} %bitcast.9, s32[8,128]{1,0:T(8,128)S(1)} %bitcast.11, f32[16,2048]{1,0:T(8,128)S(1)} %bitcast.6), custom_call_target="tpu_custom_call" | custom-call | tf_op jit(solution)/shard_map/pallas_call | solution.py:288
  87.7 0.7 copy.10
  88.3 0.6 copy.11
  89.0 0.7 copy.12
Async XLA Ops:
  0.6 2.2 %copy-start = (bf16[1024,2048]{1,0:T(8,128)(2,1)S(1)}, bf16[1024,2048]{1,0:T(8,128)(2,1)}, u32[]{:S(2)}) copy-start(bf16[1024,2048]{1,0:T(8,128)(2,1)} %e_hbm.1) | copy-start | bytes 12582916
  2.8 0.9 %copy-start.1 = (f32[2048,16]{0,1:T(8,128)S(1)}, f32[2048,16]{0,1:T(8,128)}, u32[]{:S(2)}) copy-start(f32[2048,16]{0,1:T(8,128)} %param.7) | copy-start | bytes 393220
  3.7 0.8 copy-start.2
  4.6 0.7 copy-start.3

commit v2 on v1

v2 whole, which is shorter than its diff:
```python
import functools

import jax
import jax.numpy as jnp
from jax import lax
from jax.experimental import pallas as pl
from jax.experimental.pallas import tpu as pltpu
from jax.sharding import PartitionSpec as P

MESH = pl.DeviceIdType.MESH
BF16 = jnp.bfloat16
F32 = jnp.float32
huber_delta = 8.0
LANES = 128
Y_CHIPS = 4
CORES = 2
CHUNKS = 4
LAG = 2

(X1, Y1, Z1, G1, GAMMA, X2, SCAL_Y, SCAL_Z, Y2, Z2, G2, SQUARE, CORE1) = range(13)
CORE2 = CORE1 + CHUNKS
N_SEMS = CORE2 + CHUNKS


def drain(ref, sem):
    pltpu.make_async_copy(ref, ref, sem).wait()


def kernel(ny, nz, nc, resp, all_rows,
           e_hbm, t_hbm, cls_hbm, c_hbm,
           coef_out, resid_out, dir_out,
           e, t, cls, coef, cb, w, resid, lhs, g, gn,
           part, whole, crecv, xsum, yrecv, ypart, ysum, zrecv, gath,
           row_x, row_y, row_z,
           load_sem, send_sem, recv_sem, near_sem):
    rows_here, feats = e.shape
    row_tiles = rows_here // LANES
    step_rows = rows_here // CHUNKS
    step_tiles = row_tiles // CHUNKS
    quarter = feats // ny
    pieces = quarter // LANES
    nx = nc // CORES
    near = nz // 8
    here = lax.axis_index("row")
    col = lax.axis_index("col")
    y, z = lax.div(here, nz), lax.rem(here, nz)
    x, core = lax.div(col, CORES), lax.rem(col, CORES)
    my_piece = lax.rem(z, pieces)

    def far_first(n):
        return [n // 2 + ((k + 1) // 2) * (2 * (k % 2) - 1) for k in range(n - 1)]

    def at_yz(dy, dz):
        return lax.rem(y + dy + ny, ny) * nz + lax.rem(z + dz + nz, nz), col

    def at_col(dc):
        return here, lax.rem(col + dc, nc)

    other_core = (here, col + 1 - 2 * core)
    x_mates = [(here, lax.rem(x + dx, nx) * CORES + core) for dx in far_first(nx)]
    col_mates = [at_col(dc) for dc in far_first(nc)]
    spread = [(dy, dz) for dz in sorted(range(1 - pieces // 2, pieces // 2 + 1), key=lambda d: -abs(d))
              for dy in [*far_first(ny), 0] if (dy, dz) != (0, 0)]

    def send(which, src, dst, peer):
        pltpu.make_async_remote_copy(
            src_ref=src, dst_ref=dst,
            send_sem=send_sem.at[which], recv_sem=recv_sem.at[which],
            device_id=peer, device_id_type=MESH,
        ).start()

    load_c = pltpu.make_async_copy(c_hbm, coef, load_sem.at[0])
    load_t = pltpu.make_async_copy(t_hbm, t, load_sem.at[1])
    load_cls = pltpu.make_async_copy(cls_hbm, cls, load_sem.at[2])
    load_e = [pltpu.make_async_copy(
        e_hbm.at[pl.ds(k * step_rows, step_rows)], e.at[pl.ds(k * step_rows, step_rows)],
        load_sem.at[3 + k]) for k in range(CHUNKS)]
    load_c.start()
    for load in load_e:
        load.start()
    load_t.start()
    load_cls.start()

    barrier = pltpu.get_barrier_semaphore()
    near_z = [dz for k in range(near) for dz in (near - k, k - near)]
    greeted = [*x_mates, *(at_yz(dy, 0) for dy in far_first(ny)), *(at_yz(0, dz) for dz in near_z), other_core]
    for peer in greeted:
        pl.semaphore_signal(barrier, inc=1, device_id=peer, device_id_type=MESH)

    def tell(k, reach):
        for i, dz in enumerate((reach, -reach)):
            pl.semaphore_signal(near_sem.at[2 * k + i], inc=1, device_id=at_yz(0, dz), device_id_type=MESH)

    def hear(k):
        for i in range(2):
            pl.semaphore_wait(near_sem.at[2 * k + i], 1)

    def meet():
        pl.semaphore_wait(barrier, len(greeted))
        tell(0, near)

    def x_reduce(which_core, which_x, buf, left, before_send):
        def product(k):
            if buf == 0:
                load_e[k].wait()
            both = lax.dot_general(
                left[...], e[k * step_rows:(k + 1) * step_rows, :], (((1,), (1,)), ((), ())),
                preferred_element_type=F32)
            for i in range(step_tiles):
                part[buf, k * step_tiles + i] = both[:, i * LANES:(i + 1) * LANES]
            if k == 0:
                before_send()
            tiles = pl.ds(k * step_tiles, step_tiles)
            send(which_core + k, part.at[buf, tiles], crecv.at[buf, tiles], other_core)

        def pass_on(k):
            tiles = pl.ds(k * step_tiles, step_tiles)
            drain(crecv.at[buf, tiles], recv_sem.at[which_core + k])
            xsum[buf, x, tiles] = part[buf, tiles] + crecv[buf, tiles]
            for mate in x_mates:
                send(which_x, xsum.at[buf, x, tiles], xsum.at[buf, x, tiles], mate)

        for k in range(CHUNKS + LAG):
            if k < CHUNKS:
                product(k)
            if k >= LAG:
                pass_on(k - LAG)
        drain(xsum.at[buf, pl.ds(0, nx - 1)], recv_sem.at[which_x])

    def x_total(buf, j):
        total = xsum[buf, 0, j]
        for k in range(1, nx):
            total = total + xsum[buf, k, j]
        return total

    def y_reduce(which, buf):
        for dy in [*far_first(ny), 0]:
            other = lax.rem(y + dy, ny)
            lanes = pl.ds(pl.multiple_of(other * quarter, quarter), quarter)
            both = jnp.dot(lhs[...], e[:, lanes], preferred_element_type=F32)
            total = both[:resp] + both[resp:]
            into = ypart.at[buf, other] if dy else yrecv.at[buf, y]
            for p in range(pieces):
                into[p] = total[:, p * LANES:(p + 1) * LANES]
            if dy:
                send(which, ypart.at[buf, other], yrecv.at[buf, y], at_yz(dy, 0))

    def z_reduce(which_y, which_z, buf):
        drain(yrecv.at[buf, pl.ds(0, ny - 1)], recv_sem.at[which_y])
        total = yrecv[buf, 0]
        for k in range(1, ny):
            total = total + yrecv[buf, k]
        ysum[buf] = total
        for dz in far_first(nz):
            peer_piece = lax.rem(z + dz, pieces)
            send(which_z, ysum.at[buf, peer_piece], zrecv.at[buf, z], at_yz(0, dz))
        zrecv[buf, z] = ysum[buf, my_piece]

    def spread_out(which_z, which_g, buf):
        drain(zrecv.at[buf, pl.ds(0, nz - 1)], recv_sem.at[which_z])
        total = zrecv[buf, 0]
        for k in range(1, nz):
            total = total + zrecv[buf, k]
        gath[buf, y, my_piece] = total
        for dy, dz in spread:
            send(which_g, gath.at[buf, y, my_piece], gath.at[buf, y, my_piece], at_yz(dy, dz))

    def collect(which_g, buf):
        drain(zrecv.at[buf, pl.ds(0, ny * pieces - 1)], recv_sem.at[which_g])

    lane = lax.broadcasted_iota(jnp.int32, (resp, LANES), 1)
    sub = lax.broadcasted_iota(jnp.int32, (resp, LANES), 0)
    diagonal = lane == sub

    def to_row(column):
        return jnp.sum(jnp.where(diagonal, column, 0.0), axis=0, keepdims=True)

    def to_column(row):
        return jnp.sum(jnp.where(diagonal, row, 0.0), axis=1, keepdims=True)

    load_c.wait()
    cb[...] = coef[...].astype(BF16)
    x_reduce(CORE1, X1, 0, cb, meet)
    load_t.wait()
    load_cls.wait()
    hear(0)
    tell(1, 2 * near)

    def put_pair(j, value):
        high = value.astype(BF16)
        low = (value - high.astype(F32)).astype(BF16)
        lanes = slice(j * LANES, (j + 1) * LANES)
        lhs[0:resp, lanes] = high
        lhs[resp:2 * resp, lanes] = low

    for j in range(row_tiles):
        r = t[:, j * LANES:(j + 1) * LANES] - x_total(0, j)
        resid[j] = r
        norm = jnp.sqrt(jnp.sum(r * r, axis=0, keepdims=True))
        weight = jnp.where(
            cls[j:j + 1, :] == 1, huber_delta / jnp.maximum(huber_delta, norm), 1.0)
        w[j:j + 1, :] = weight
        put_pair(j, weight * r)

    y_reduce(Y1, 0)
    hear(1)
    z_reduce(Y1, Z1, 0)
    spread_out(Z1, G1, 0)
    collect(G1, 0)
    norm2 = jnp.zeros((resp, LANES), F32)
    for other in range(ny):
        for p in range(pieces):
            piece = gath[0, other, p]
            lanes = slice(other * quarter + p * LANES, other * quarter + (p + 1) * LANES)
            g[:, lanes] = piece
            cb[:, lanes] = piece.astype(BF16)
            norm2 = norm2 + piece * piece
    row_x[0, col] = to_row(jnp.sum(norm2, axis=1, keepdims=True))
    for mate in col_mates:
        send(GAMMA, row_x.at[0, col], row_x.at[0, col], mate)

    x_reduce(CORE2, X2, 1, cb, lambda: None)
    curv = jnp.zeros((resp, LANES), F32)
    weight_sum = jnp.zeros((1, LANES), F32)
    for j in range(row_tiles):
        weight = w[j:j + 1, :]
        image = x_total(1, j)
        whole[j] = image
        scaled = weight * image
        curv = curv + scaled * image
        weight_sum = weight_sum + weight
        put_pair(j, scaled)
    row_y[y] = to_row(jnp.sum(curv, axis=1, keepdims=True)) + jnp.where(
        lane[0:1] == resp, jnp.sum(weight_sum, axis=1, keepdims=True), 0.0)
    for dy in far_first(ny):
        send(SCAL_Y, row_y.at[y], row_y.at[y], at_yz(dy, 0))

    y_reduce(Y2, 1)
    drain(row_y.at[pl.ds(0, ny - 1)], recv_sem.at[SCAL_Y])
    row_z[z] = jnp.sum(row_y[...], axis=0)
    for dz in far_first(nz):
        send(SCAL_Z, row_z.at[z], row_z.at[z], at_yz(0, dz))
    z_reduce(Y2, Z2, 1)

    drain(row_x.at[0, pl.ds(0, nc - 1)], recv_sem.at[GAMMA])
    drain(row_z.at[pl.ds(0, nz - 1)], recv_sem.at[SCAL_Z])
    sums = jnp.sum(row_z[...], axis=0)
    gamma_raw = to_column(jnp.sum(row_x[0], axis=0))
    curv_raw = to_column(sums)
    mean = jnp.sum(jnp.where(lane[0:1] == resp, sums, 0.0), axis=1, keepdims=True) / all_rows
    gamma = gamma_raw / (mean * mean)
    alpha = gamma / (curv_raw / (mean * mean * mean))
    ratio = alpha / mean
    coef_out[...] = coef[...] + alpha * (g[...] / mean)
    for j in range(row_tiles):
        resid_out[:, j * LANES:(j + 1) * LANES] = resid[j] - alpha * (whole[j] / mean)
    spread_out(Z2, G2, 1)
    collect(G2, 1)

    norm2 = jnp.zeros((resp, LANES), F32)
    for other in range(ny):
        for p in range(pieces):
            lanes = slice(other * quarter + p * LANES, other * quarter + (p + 1) * LANES)
            piece = g[:, lanes] - ratio * gath[1, other, p]
            gn[:, lanes] = piece
            norm2 = norm2 + piece * piece
    row_x[1, col] = to_row(jnp.sum(norm2, axis=1, keepdims=True))
    for mate in col_mates:
        send(SQUARE, row_x.at[1, col], row_x.at[1, col], mate)
    drain(row_x.at[1, pl.ds(0, nc - 1)], recv_sem.at[SQUARE])
    square = to_column(jnp.sum(row_x[1], axis=0))
    beta = square / (mean * mean) / gamma
    dir_out[...] = gn[...] / mean + beta * (g[...] / mean)

    for which, ref in (
        (X1, xsum.at[0, pl.ds(0, nx - 1)]), (X2, xsum.at[1, pl.ds(0, nx - 1)]),
        (Y1, yrecv.at[0, pl.ds(0, ny - 1)]), (Y2, yrecv.at[1, pl.ds(0, ny - 1)]),
        (Z1, zrecv.at[0, pl.ds(0, nz - 1)]), (Z2, zrecv.at[1, pl.ds(0, nz - 1)]),
        (G1, zrecv.at[0, pl.ds(0, ny * pieces - 1)]), (G2, zrecv.at[1, pl.ds(0, ny * pieces - 1)]),
        (GAMMA, row_x.at[0, pl.ds(0, nc - 1)]), (SQUARE, row_x.at[1, pl.ds(0, nc - 1)]),
        (SCAL_Y, row_y.at[pl.ds(0, ny - 1)]), (SCAL_Z, row_z.at[pl.ds(0, nz - 1)]),
        *((base + k, crecv.at[0, pl.ds(0, step_tiles)]) for base in (CORE1, CORE2) for k in range(CHUNKS)),
    ):
        drain(ref, send_sem.at[which])


def write_out(a_in, b_in, c_in, a_out, b_out, c_out, sems):
    copies = [pltpu.make_async_copy(src, dst, sems.at[k])
              for k, (src, dst) in enumerate(((a_in, a_out), (b_in, b_out), (c_in, c_out)))]
    for copy in copies:
        copy.start()
    for copy in copies:
        copy.wait()


def shards(ny, embeddings, targets, classes, start_coef):
    rows_here, feats = embeddings.shape
    resp = targets.shape[1]
    all_rows = rows_here * lax.axis_size("row")
    nc = lax.axis_size("col")
    nz = lax.axis_size("row") // ny
    row_tiles = rows_here // LANES
    pieces = feats // ny // LANES
    vmem = pltpu.VMEM
    outs = (
        jax.ShapeDtypeStruct((resp, feats), F32),
        jax.ShapeDtypeStruct((resp, rows_here), F32),
        jax.ShapeDtypeStruct((resp, feats), F32),
    )
    results = pl.pallas_call(
        functools.partial(kernel, ny, nz, nc, resp, float(all_rows)),
        out_shape=outs,
        in_specs=[pl.BlockSpec(memory_space=pl.ANY)] * 4,
        out_specs=(pl.BlockSpec(memory_space=pltpu.VMEM),) * 3,
        scratch_shapes=[
            vmem((rows_here, feats), BF16),
            vmem((resp, rows_here), F32),
            vmem((row_tiles, LANES), jnp.int32),
            vmem((resp, feats), F32),
            vmem((resp, feats), BF16),
            vmem((row_tiles, LANES), F32),
            vmem((row_tiles, resp, LANES), F32),
            vmem((2 * resp, rows_here), BF16),
            vmem((resp, feats), F32),
            vmem((resp, feats), F32),
            vmem((2, row_tiles, resp, LANES), F32),
            vmem((row_tiles, resp, LANES), F32),
            vmem((2, row_tiles, resp, LANES), F32),
            vmem((2, nc // CORES, row_tiles, resp, LANES), F32),
            vmem((2, ny, pieces, resp, LANES), F32),
            vmem((2, ny, pieces, resp, LANES), F32),
            vmem((2, pieces, resp, LANES), F32),
            vmem((2, max(nz, ny * pieces), resp, LANES), F32),
            vmem((2, ny, pieces, resp, LANES), F32),
            vmem((2, nc, 1, LANES), F32),
            vmem((ny, 1, LANES), F32),
            vmem((nz, 1, LANES), F32),
            pltpu.SemaphoreType.DMA((3 + CHUNKS,)),
            pltpu.SemaphoreType.DMA((N_SEMS,)),
            pltpu.SemaphoreType.DMA((N_SEMS,)),
            pltpu.SemaphoreType.REGULAR((4,)),
        ],
        compiler_params=pltpu.CompilerParams(
            collective_id=0, has_side_effects=True, vmem_limit_bytes=60 * 1024 * 1024),
    )(embeddings, targets.T, classes.reshape(row_tiles, LANES), start_coef.T)
    results = pl.pallas_call(
        write_out,
        out_shape=outs,
        in_specs=[pl.BlockSpec(memory_space=pl.ANY)] * 3,
        out_specs=(pl.BlockSpec(memory_space=pl.ANY),) * 3,
        scratch_shapes=[pltpu.SemaphoreType.DMA((3,))],
    )(*results)
    return tuple(out.T for out in results)


def solution(mesh, y_chips=Y_CHIPS):
    return jax.shard_map(
        functools.partial(shards, y_chips),
        mesh=mesh,
        in_specs=(P("row", "col"), P("row", None), P("row"), P("col", None)),
        out_specs=(P("col", None), P("row", None), P("col", None)),
        check_vma=False,
    )
```

time: 89.9 us -> 80.1 us (0.89)
  local copies, waits for them, and re-layouts: 6.55 us -> 0 us
  Pallas kernels: 82.4 us -> 79.3 us
    pallas_call x1, Pallas kernels: 82.4 us -> 68.3 us  [shards(): pl.pallas_call(functools.partial(kernel, ny, nz, nc, resp, float(all_rows...]
    pallas_call x0 -> x1, Pallas kernels: none -> 11.1 us  [shards(): pl.pallas_call(write_out, out_shape=outs, in_specs=[pl.BlockSpec(memory_s...]
    unnamed x11 -> x0, local copies, waits for them, and re-layouts: 6.55 us -> none
where the time goes in v2:
time: 80.1 us; the launch traced here: 80 us
  Pallas kernels  79.3 us (99%)
    pallas_call x1, Pallas kernels, shards(): pl.pallas_call(functools.partial(kernel, ny, nz, nc, resp, float(all_rows...  68.3 us
    pallas_call x1, Pallas kernels, shards(): pl.pallas_call(write_out, out_shape=outs, in_specs=[pl.BlockSpec(memory_s...  11.1 us

profile of v2, /device:TPU:1, one launch (start us, length us, event | category | flops | bytes accessed | tf_op | source)
XLA Modules:
  0.0 80.0 jit_solution(13567153781691139113)
XLA Ops:
  0.6 68.3 %shard_map.67 = (f32[16,2048]{1,0:T(8,128)}, f32[16,1024]{1,0:T(8,128)}, f32[16,2048]{1,0:T(8,128)}) custom-call(bf16[1024,2048]{1,0:T(8,128)(2,1)} %e_hbm.1, f32[16,1024]{1,0:T(8,128)} %bitcast.7, s32[8,128]{1,0:T(8,128)} %bitcast.8, f32[16,2048]{1,0:T(8,128)} %bitcast.6), custom_call_target="tpu_custom_call" | custom-call | tf_op jit(solution)/shard_map/pallas_call | solution.py:310
  68.9 11.1 %shard_map.68 = (f32[16,2048]{1,0:T(8,128)}, f32[16,1024]{1,0:T(8,128)}, f32[16,2048]{1,0:T(8,128)}) custom-call(f32[16,2048]{1,0:T(8,128)} %get-tuple-element.9.a_in, f32[16,1024]{1,0:T(8,128)} %get-tuple-element.10.b_in, f32[16,2048]{1,0:T(8,128)} %get-tuple-element.11.c_in), custom_call_target="tpu_custom_call" | custom-call | tf_op jit(solution)/shard_map/pallas_call | solution.py:346

commit v3 on v2

--- a/solution.py
+++ b/solution.py
@@ -14,12 +14,15 @@
 LANES = 128
 Y_CHIPS = 4
 CORES = 2
-CHUNKS = 4
-LAG = 2
-
-(X1, Y1, Z1, G1, GAMMA, X2, SCAL_Y, SCAL_Z, Y2, Z2, G2, SQUARE, CORE1) = range(13)
+CHUNKS = 2
+
+(Y1, Z1, GAMMA, SCAL_Y, SCAL_Z, Y2, Z2, SQUARE, CORE1) = range(9)
 CORE2 = CORE1 + CHUNKS
-N_SEMS = CORE2 + CHUNKS
+X1 = CORE2 + CHUNKS
+X2 = X1 + CHUNKS
+G1 = X2 + CHUNKS
+G2 = G1 + Y_CHIPS
+N_SEMS = G2 + Y_CHIPS
 
 
 def drain(ref, sem):
@@ -29,7 +32,7 @@
 def kernel(ny, nz, nc, resp, all_rows,
            e_hbm, t_hbm, cls_hbm, c_hbm,
            coef_out, resid_out, dir_out,
-           e, t, cls, coef, cb, w, resid, lhs, g, gn,
+           e, t, cls, coef, cb, acc, gacc, w, resid, lhs, g, gn,
            part, whole, crecv, xsum, yrecv, ypart, ysum, zrecv, gath,
            row_x, row_y, row_z,
            load_sem, send_sem, recv_sem, near_sem):
@@ -99,33 +102,37 @@
         pl.semaphore_wait(barrier, len(greeted))
         tell(0, near)
 
-    def x_reduce(which_core, which_x, buf, left, before_send):
-        def product(k):
-            if buf == 0:
-                load_e[k].wait()
-            both = lax.dot_general(
-                left[...], e[k * step_rows:(k + 1) * step_rows, :], (((1,), (1,)), ((), ())),
-                preferred_element_type=F32)
+    def x_send(which_core, which_x, buf, product, before_send, between):
+        for k in range(CHUNKS):
+            both = product(slice(k * step_rows, (k + 1) * step_rows), k)
             for i in range(step_tiles):
                 part[buf, k * step_tiles + i] = both[:, i * LANES:(i + 1) * LANES]
             if k == 0:
                 before_send()
             tiles = pl.ds(k * step_tiles, step_tiles)
             send(which_core + k, part.at[buf, tiles], crecv.at[buf, tiles], other_core)
-
-        def pass_on(k):
+        between()
+        for k in range(CHUNKS):
             tiles = pl.ds(k * step_tiles, step_tiles)
             drain(crecv.at[buf, tiles], recv_sem.at[which_core + k])
             xsum[buf, x, tiles] = part[buf, tiles] + crecv[buf, tiles]
             for mate in x_mates:
-                send(which_x, xsum.at[buf, x, tiles], xsum.at[buf, x, tiles], mate)
-
-        for k in range(CHUNKS + LAG):
-            if k < CHUNKS:
-                product(k)
-            if k >= LAG:
-                pass_on(k - LAG)
-        drain(xsum.at[buf, pl.ds(0, nx - 1)], recv_sem.at[which_x])
+                send(which_x + k, xsum.at[buf, x, tiles], xsum.at[buf, x, tiles], mate)
+
+    def against_rows(left, rows, lanes):
+        return lax.dot_general(
+            left, e[rows, lanes], (((1,), (1,)), ((), ())), preferred_element_type=F32)
+
+    def x_chunks(which_x, buf, of_tile):
+        for k in range(CHUNKS):
+            drain(xsum.at[buf, pl.ds(0, nx - 1), pl.ds(0, step_tiles)], recv_sem.at[which_x + k])
+            for j in range(k * step_tiles, (k + 1) * step_tiles):
+                of_tile(j)
+            if k < CHUNKS - 1:
+                rows = slice(k * step_rows, (k + 1) * step_rows)
+                both = jnp.dot(lhs[:, rows], e[rows, :], preferred_element_type=F32)
+                total = both[:resp] + both[resp:]
+                gacc[...] = total if k == 0 else gacc[...] + total
 
     def x_total(buf, j):
         total = xsum[buf, 0, j]
@@ -137,8 +144,9 @@
         for dy in [*far_first(ny), 0]:
             other = lax.rem(y + dy, ny)
             lanes = pl.ds(pl.multiple_of(other * quarter, quarter), quarter)
-            both = jnp.dot(lhs[...], e[:, lanes], preferred_element_type=F32)
-            total = both[:resp] + both[resp:]
+            rows = slice((CHUNKS - 1) * step_rows, CHUNKS * step_rows)
+            both = jnp.dot(lhs[:, rows], e[rows, lanes], preferred_element_type=F32)
+            total = gacc[:, lanes] + both[:resp] + both[resp:]
             into = ypart.at[buf, other] if dy else yrecv.at[buf, y]
             for p in range(pieces):
                 into[p] = total[:, p * LANES:(p + 1) * LANES]
@@ -163,10 +171,13 @@
             total = total + zrecv[buf, k]
         gath[buf, y, my_piece] = total
         for dy, dz in spread:
-            send(which_g, gath.at[buf, y, my_piece], gath.at[buf, y, my_piece], at_yz(dy, dz))
-
-    def collect(which_g, buf):
-        drain(zrecv.at[buf, pl.ds(0, ny * pieces - 1)], recv_sem.at[which_g])
+            send(which_g + dy, gath.at[buf, y, my_piece], gath.at[buf, y, my_piece], at_yz(dy, dz))
+
+    def collect(which_g, buf, dy):
+        drain(zrecv.at[buf, pl.ds(0, pieces if dy else pieces - 1)], recv_sem.at[which_g + dy])
+        return lax.rem(y - dy + ny, ny)
+
+    by_arrival = [0, *reversed(far_first(ny))]
 
     lane = lax.broadcasted_iota(jnp.int32, (resp, LANES), 1)
     sub = lax.broadcasted_iota(jnp.int32, (resp, LANES), 0)
@@ -180,7 +191,12 @@
 
     load_c.wait()
     cb[...] = coef[...].astype(BF16)
-    x_reduce(CORE1, X1, 0, cb, meet)
+
+    def first_product(rows, k):
+        load_e[k].wait()
+        return against_rows(cb[...], rows, slice(None))
+
+    x_send(CORE1, X1, 0, first_product, meet, lambda: None)
     load_t.wait()
     load_cls.wait()
     hear(0)
@@ -193,7 +209,7 @@
         lhs[0:resp, lanes] = high
         lhs[resp:2 * resp, lanes] = low
 
-    for j in range(row_tiles):
+    def weigh(j):
         r = t[:, j * LANES:(j + 1) * LANES] - x_total(0, j)
         resid[j] = r
         norm = jnp.sqrt(jnp.sum(r * r, axis=0, keepdims=True))
@@ -202,34 +218,50 @@
         w[j:j + 1, :] = weight
         put_pair(j, weight * r)
 
+    x_chunks(X1, 0, weigh)
+
     y_reduce(Y1, 0)
     hear(1)
     z_reduce(Y1, Z1, 0)
     spread_out(Z1, G1, 0)
-    collect(G1, 0)
-    norm2 = jnp.zeros((resp, LANES), F32)
-    for other in range(ny):
+    for k, dy in enumerate(by_arrival):
+        behind = collect(G1, 0, dy)
         for p in range(pieces):
-            piece = gath[0, other, p]
-            lanes = slice(other * quarter + p * LANES, other * quarter + (p + 1) * LANES)
+            lanes = pl.ds(pl.multiple_of(behind * quarter + p * LANES, LANES), LANES)
+            piece = gath[0, behind, p]
             g[:, lanes] = piece
             cb[:, lanes] = piece.astype(BF16)
+        lanes = pl.ds(pl.multiple_of(behind * quarter, quarter), quarter)
+        if k < ny - 1:
+            share = against_rows(cb[:, lanes], slice(None), lanes)
+            acc[...] = share if k == 0 else acc[...] + share
+
+    def last_product(rows, k):
+        return acc[:, rows] + against_rows(cb[:, lanes], rows, lanes)
+
+    def send_gamma():
+        norm2 = jnp.zeros((resp, LANES), F32)
+        for p in range(ny * pieces):
+            piece = g[:, p * LANES:(p + 1) * LANES]
             norm2 = norm2 + piece * piece
-    row_x[0, col] = to_row(jnp.sum(norm2, axis=1, keepdims=True))
-    for mate in col_mates:
-        send(GAMMA, row_x.at[0, col], row_x.at[0, col], mate)
-
-    x_reduce(CORE2, X2, 1, cb, lambda: None)
-    curv = jnp.zeros((resp, LANES), F32)
-    weight_sum = jnp.zeros((1, LANES), F32)
-    for j in range(row_tiles):
+        row_x[0, col] = to_row(jnp.sum(norm2, axis=1, keepdims=True))
+        for mate in col_mates:
+            send(GAMMA, row_x.at[0, col], row_x.at[0, col], mate)
+
+    x_send(CORE2, X2, 1, last_product, lambda: None, send_gamma)
+    sums = [jnp.zeros((resp, LANES), F32), jnp.zeros((1, LANES), F32)]
+
+    def weigh_image(j):
         weight = w[j:j + 1, :]
         image = x_total(1, j)
         whole[j] = image
         scaled = weight * image
-        curv = curv + scaled * image
-        weight_sum = weight_sum + weight
+        sums[0] = sums[0] + scaled * image
+        sums[1] = sums[1] + weight
         put_pair(j, scaled)
+
+    x_chunks(X2, 1, weigh_image)
+    curv, weight_sum = sums
     row_y[y] = to_row(jnp.sum(curv, axis=1, keepdims=True)) + jnp.where(
         lane[0:1] == resp, jnp.sum(weight_sum, axis=1, keepdims=True), 0.0)
     for dy in far_first(ny):
@@ -255,7 +287,8 @@
     for j in range(row_tiles):
         resid_out[:, j * LANES:(j + 1) * LANES] = resid[j] - alpha * (whole[j] / mean)
     spread_out(Z2, G2, 1)
-    collect(G2, 1)
+    for dy in by_arrival:
+        collect(G2, 1, dy)
 
     norm2 = jnp.zeros((resp, LANES), F32)
     for other in range(ny):
@@ -273,13 +306,13 @@
     dir_out[...] = gn[...] / mean + beta * (g[...] / mean)
 
     for which, ref in (
-        (X1, xsum.at[0, pl.ds(0, nx - 1)]), (X2, xsum.at[1, pl.ds(0, nx - 1)]),
         (Y1, yrecv.at[0, pl.ds(0, ny - 1)]), (Y2, yrecv.at[1, pl.ds(0, ny - 1)]),
         (Z1, zrecv.at[0, pl.ds(0, nz - 1)]), (Z2, zrecv.at[1, pl.ds(0, nz - 1)]),
-        (G1, zrecv.at[0, pl.ds(0, ny * pieces - 1)]), (G2, zrecv.at[1, pl.ds(0, ny * pieces - 1)]),
         (GAMMA, row_x.at[0, pl.ds(0, nc - 1)]), (SQUARE, row_x.at[1, pl.ds(0, nc - 1)]),
         (SCAL_Y, row_y.at[pl.ds(0, ny - 1)]), (SCAL_Z, row_z.at[pl.ds(0, nz - 1)]),
         *((base + k, crecv.at[0, pl.ds(0, step_tiles)]) for base in (CORE1, CORE2) for k in range(CHUNKS)),
+        *((base + k, xsum.at[0, pl.ds(0, nx - 1), pl.ds(0, step_tiles)]) for base in (X1, X2) for k in range(CHUNKS)),
+        *((base + k, zrecv.at[0, pl.ds(0, pieces if k else pieces - 1)]) for base in (G1, G2) for k in range(ny)),
     ):
         drain(ref, send_sem.at[which])
 
@@ -310,7 +343,7 @@
     results = pl.pallas_call(
         functools.partial(kernel, ny, nz, nc, resp, float(all_rows)),
         out_shape=outs,
-        in_specs=[pl.BlockSpec(memory_space=pl.ANY)] * 4,
+        in_specs=[pl.BlockSpec(memory_space=pltpu.HBM)] * 4,
         out_specs=(pl.BlockSpec(memory_space=pltpu.VMEM),) * 3,
         scratch_shapes=[
             vmem((rows_here, feats), BF16),
@@ -318,6 +351,8 @@
             vmem((row_tiles, LANES), jnp.int32),
             vmem((resp, feats), F32),
             vmem((resp, feats), BF16),
+            vmem((resp, rows_here), F32),
+            vmem((resp, feats), F32),
             vmem((row_tiles, LANES), F32),
             vmem((row_tiles, resp, LANES), F32),
             vmem((2 * resp, rows_here), BF16),
@@ -346,9 +381,10 @@
     results = pl.pallas_call(
         write_out,
         out_shape=outs,
-        in_specs=[pl.BlockSpec(memory_space=pl.ANY)] * 3,
+        in_specs=[pl.BlockSpec(memory_space=pltpu.VMEM)] * 3,
         out_specs=(pl.BlockSpec(memory_space=pl.ANY),) * 3,
         scratch_shapes=[pltpu.SemaphoreType.DMA((3,))],
+        compiler_params=pltpu.CompilerParams(vmem_limit_bytes=60 * 1024 * 1024),
     )(*results)
     return tuple(out.T for out in results)
 

time: 80.1 us -> 70.6 us (0.88)
  Pallas kernels: 79.3 us -> 69.8 us
    pallas_call x1, Pallas kernels: 11.1 us -> 1.75 us  [shards(): pl.pallas_call(write_out, out_shape=outs, in_specs=[pl.BlockSpec(memory_s...]
where the time goes in v3:
time: 70.6 us; the launch traced here: 70.5 us
  Pallas kernels  69.8 us (99%)
    pallas_call x1, Pallas kernels, shards(): pl.pallas_call(functools.partial(kernel, ny, nz, nc, resp, float(all_rows...  68.1 us
    pallas_call x1, Pallas kernels, shards(): pl.pallas_call(write_out, out_shape=outs, in_specs=[pl.BlockSpec(memory_s...  1.75 us

profile of v3, /device:TPU:1, one launch (start us, length us, event | category | flops | bytes accessed | tf_op | source)
XLA Modules:
  0.0 70.5 jit_solution(10741019523768146523)
XLA Ops:
  0.6 68.1 %shard_map.67 = (f32[16,2048]{1,0:T(8,128)}, f32[16,1024]{1,0:T(8,128)}, f32[16,2048]{1,0:T(8,128)}) custom-call(bf16[1024,2048]{1,0:T(8,128)(2,1)} %e_hbm.1, f32[16,1024]{1,0:T(8,128)} %bitcast.7, s32[8,128]{1,0:T(8,128)} %bitcast.8, f32[16,2048]{1,0:T(8,128)} %bitcast.6), custom_call_target="tpu_custom_call" | custom-call | tf_op jit(solution)/shard_map/pallas_call | solution.py:343
  68.7 1.8 %shard_map.68 = (f32[16,2048]{1,0:T(8,128)}, f32[16,1024]{1,0:T(8,128)}, f32[16,2048]{1,0:T(8,128)}) custom-call(f32[16,2048]{1,0:T(8,128)} %get-tuple-element.9.a_in, f32[16,1024]{1,0:T(8,128)} %get-tuple-element.10.b_in, f32[16,2048]{1,0:T(8,128)} %get-tuple-element.11.c_in), custom_call_target="tpu_custom_call" | custom-call | tf_op jit(solution)/shard_map/pallas_call | solution.py:381

commit v4 on v3

--- a/solution.py
+++ b/solution.py
@@ -14,13 +14,8 @@
 LANES = 128
 Y_CHIPS = 4
 CORES = 2
-CHUNKS = 2
-
-(Y1, Z1, GAMMA, SCAL_Y, SCAL_Z, Y2, Z2, SQUARE, CORE1) = range(9)
-CORE2 = CORE1 + CHUNKS
-X1 = CORE2 + CHUNKS
-X2 = X1 + CHUNKS
-G1 = X2 + CHUNKS
+
+(CORE1, X1, BACK1, Y1, Z1, GAMMA, CORE2, X2, BACK2, SCAL_Y, SCAL_Z, Y2, Z2, SQUARE, G1) = range(15)
 G2 = G1 + Y_CHIPS
 N_SEMS = G2 + Y_CHIPS
 
@@ -32,14 +27,14 @@
 def kernel(ny, nz, nc, resp, all_rows,
            e_hbm, t_hbm, cls_hbm, c_hbm,
            coef_out, resid_out, dir_out,
-           e, t, cls, coef, cb, acc, gacc, w, resid, lhs, g, gn,
-           part, whole, crecv, xsum, yrecv, ypart, ysum, zrecv, gath,
-           row_x, row_y, row_z,
+           e, t, cls, coef, cb, acc, gacc, w, resid, lhs, g,
+           part, crecv, xsum, xfull, yrecv, ypart, ysum, zrecv, gath,
+           row_x, row_y, row_z, row_sq,
            load_sem, send_sem, recv_sem, near_sem):
     rows_here, feats = e.shape
     row_tiles = rows_here // LANES
-    step_rows = rows_here // CHUNKS
-    step_tiles = row_tiles // CHUNKS
+    half_rows = rows_here // CORES
+    half_tiles = row_tiles // CORES
     quarter = feats // ny
     pieces = quarter // LANES
     nx = nc // CORES
@@ -49,6 +44,16 @@
     y, z = lax.div(here, nz), lax.rem(here, nz)
     x, core = lax.div(col, CORES), lax.rem(col, CORES)
     my_piece = lax.rem(z, pieces)
+    theirs = 1 - core
+
+    def tile_at(j):
+        return pl.ds(pl.multiple_of(j * LANES, LANES), LANES)
+
+    def rows_of(k):
+        return pl.ds(pl.multiple_of(k * half_rows, half_rows), half_rows)
+
+    def tiles_of(k):
+        return pl.ds(k * half_tiles, half_tiles)
 
     def far_first(n):
         return [n // 2 + ((k + 1) // 2) * (2 * (k % 2) - 1) for k in range(n - 1)]
@@ -76,8 +81,7 @@
     load_t = pltpu.make_async_copy(t_hbm, t, load_sem.at[1])
     load_cls = pltpu.make_async_copy(cls_hbm, cls, load_sem.at[2])
     load_e = [pltpu.make_async_copy(
-        e_hbm.at[pl.ds(k * step_rows, step_rows)], e.at[pl.ds(k * step_rows, step_rows)],
-        load_sem.at[3 + k]) for k in range(CHUNKS)]
+        e_hbm.at[rows_of(k)], e.at[rows_of(k)], load_sem.at[3 + i]) for i, k in enumerate((theirs, core))]
     load_c.start()
     for load in load_e:
         load.start()
@@ -102,50 +106,45 @@
         pl.semaphore_wait(barrier, len(greeted))
         tell(0, near)
 
-    def x_send(which_core, which_x, buf, product, before_send, between):
-        for k in range(CHUNKS):
-            both = product(slice(k * step_rows, (k + 1) * step_rows), k)
-            for i in range(step_tiles):
-                part[buf, k * step_tiles + i] = both[:, i * LANES:(i + 1) * LANES]
-            if k == 0:
-                before_send()
-            tiles = pl.ds(k * step_tiles, step_tiles)
-            send(which_core + k, part.at[buf, tiles], crecv.at[buf, tiles], other_core)
-        between()
-        for k in range(CHUNKS):
-            tiles = pl.ds(k * step_tiles, step_tiles)
-            drain(crecv.at[buf, tiles], recv_sem.at[which_core + k])
-            xsum[buf, x, tiles] = part[buf, tiles] + crecv[buf, tiles]
-            for mate in x_mates:
-                send(which_x + k, xsum.at[buf, x, tiles], xsum.at[buf, x, tiles], mate)
-
     def against_rows(left, rows, lanes):
         return lax.dot_general(
             left, e[rows, lanes], (((1,), (1,)), ((), ())), preferred_element_type=F32)
 
-    def x_chunks(which_x, buf, of_tile):
-        for k in range(CHUNKS):
-            drain(xsum.at[buf, pl.ds(0, nx - 1), pl.ds(0, step_tiles)], recv_sem.at[which_x + k])
-            for j in range(k * step_tiles, (k + 1) * step_tiles):
-                of_tile(j)
-            if k < CHUNKS - 1:
-                rows = slice(k * step_rows, (k + 1) * step_rows)
-                both = jnp.dot(lhs[:, rows], e[rows, :], preferred_element_type=F32)
-                total = both[:resp] + both[resp:]
-                gacc[...] = total if k == 0 else gacc[...] + total
-
-    def x_total(buf, j):
-        total = xsum[buf, 0, j]
+    def x_reduce(which_core, which_x, which_back, buf, product, before_send, between):
+        for i, k in enumerate((theirs, core)):
+            both = product(rows_of(k), i)
+            for j in range(half_tiles):
+                part[buf, k * half_tiles + j] = both[:, j * LANES:(j + 1) * LANES]
+            if i == 0:
+                before_send()
+                send(which_core, part.at[buf, tiles_of(k)], crecv.at[buf], other_core)
+        between()
+        drain(crecv.at[buf], recv_sem.at[which_core])
+        xsum[buf, x] = part[buf, tiles_of(core)] + crecv[buf]
+        for mate in x_mates:
+            send(which_x, xsum.at[buf, x], xsum.at[buf, x], mate)
+        drain(xsum.at[buf, pl.ds(0, nx - 1)], recv_sem.at[which_x])
+        total = xsum[buf, 0]
         for k in range(1, nx):
-            total = total + xsum[buf, k, j]
-        return total
+            total = total + xsum[buf, k]
+        xfull[buf, tiles_of(core)] = total
+        send(which_back, xfull.at[buf, tiles_of(core)], xfull.at[buf, tiles_of(core)], other_core)
+
+    def x_halves(which_back, buf, of_tile):
+        for i, k in enumerate((core, theirs)):
+            if i == 1:
+                drain(crecv.at[buf], recv_sem.at[which_back])
+            for j in range(half_tiles):
+                of_tile(i, k * half_tiles + j)
+            if i == 0:
+                both = jnp.dot(lhs[:, rows_of(k)], e[rows_of(k), :], preferred_element_type=F32)
+                gacc[...] = both[:resp] + both[resp:]
 
     def y_reduce(which, buf):
         for dy in [*far_first(ny), 0]:
             other = lax.rem(y + dy, ny)
             lanes = pl.ds(pl.multiple_of(other * quarter, quarter), quarter)
-            rows = slice((CHUNKS - 1) * step_rows, CHUNKS * step_rows)
-            both = jnp.dot(lhs[:, rows], e[rows, lanes], preferred_element_type=F32)
+            both = jnp.dot(lhs[:, rows_of(theirs)], e[rows_of(theirs), lanes], preferred_element_type=F32)
             total = gacc[:, lanes] + both[:resp] + both[resp:]
             into = ypart.at[buf, other] if dy else yrecv.at[buf, y]
             for p in range(pieces):
@@ -164,14 +163,16 @@
             send(which_z, ysum.at[buf, peer_piece], zrecv.at[buf, z], at_yz(0, dz))
         zrecv[buf, z] = ysum[buf, my_piece]
 
-    def spread_out(which_z, which_g, buf):
+    def spread_out(which_z, which_g, buf, change):
         drain(zrecv.at[buf, pl.ds(0, nz - 1)], recv_sem.at[which_z])
         total = zrecv[buf, 0]
         for k in range(1, nz):
             total = total + zrecv[buf, k]
+        total = change(total)
         gath[buf, y, my_piece] = total
         for dy, dz in spread:
             send(which_g + dy, gath.at[buf, y, my_piece], gath.at[buf, y, my_piece], at_yz(dy, dz))
+        return total
 
     def collect(which_g, buf, dy):
         drain(zrecv.at[buf, pl.ds(0, pieces if dy else pieces - 1)], recv_sem.at[which_g + dy])
@@ -192,11 +193,11 @@
     load_c.wait()
     cb[...] = coef[...].astype(BF16)
 
-    def first_product(rows, k):
-        load_e[k].wait()
+    def first_product(rows, i):
+        load_e[i].wait()
         return against_rows(cb[...], rows, slice(None))
 
-    x_send(CORE1, X1, 0, first_product, meet, lambda: None)
+    x_reduce(CORE1, X1, BACK1, 0, first_product, meet, lambda: None)
     load_t.wait()
     load_cls.wait()
     hear(0)
@@ -205,25 +206,24 @@
     def put_pair(j, value):
         high = value.astype(BF16)
         low = (value - high.astype(F32)).astype(BF16)
-        lanes = slice(j * LANES, (j + 1) * LANES)
-        lhs[0:resp, lanes] = high
-        lhs[resp:2 * resp, lanes] = low
-
-    def weigh(j):
-        r = t[:, j * LANES:(j + 1) * LANES] - x_total(0, j)
+        lhs[0:resp, tile_at(j)] = high
+        lhs[resp:2 * resp, tile_at(j)] = low
+
+    def weigh(i, j):
+        r = t[:, tile_at(j)] - xfull[0, j]
         resid[j] = r
         norm = jnp.sqrt(jnp.sum(r * r, axis=0, keepdims=True))
         weight = jnp.where(
-            cls[j:j + 1, :] == 1, huber_delta / jnp.maximum(huber_delta, norm), 1.0)
-        w[j:j + 1, :] = weight
+            cls[pl.ds(j, 1), :] == 1, huber_delta / jnp.maximum(huber_delta, norm), 1.0)
+        w[j] = weight
         put_pair(j, weight * r)
 
-    x_chunks(X1, 0, weigh)
+    x_halves(BACK1, 0, weigh)
 
     y_reduce(Y1, 0)
     hear(1)
     z_reduce(Y1, Z1, 0)
-    spread_out(Z1, G1, 0)
+    spread_out(Z1, G1, 0, lambda total: total)
     for k, dy in enumerate(by_arrival):
         behind = collect(G1, 0, dy)
         for p in range(pieces):
@@ -244,24 +244,23 @@
         for p in range(ny * pieces):
             piece = g[:, p * LANES:(p + 1) * LANES]
             norm2 = norm2 + piece * piece
-        row_x[0, col] = to_row(jnp.sum(norm2, axis=1, keepdims=True))
+        row_x[col] = to_row(jnp.sum(norm2, axis=1, keepdims=True))
         for mate in col_mates:
-            send(GAMMA, row_x.at[0, col], row_x.at[0, col], mate)
-
-    x_send(CORE2, X2, 1, last_product, lambda: None, send_gamma)
-    sums = [jnp.zeros((resp, LANES), F32), jnp.zeros((1, LANES), F32)]
-
-    def weigh_image(j):
-        weight = w[j:j + 1, :]
-        image = x_total(1, j)
-        whole[j] = image
+            send(GAMMA, row_x.at[col], row_x.at[col], mate)
+
+    x_reduce(CORE2, X2, BACK2, 1, last_product, lambda: None, send_gamma)
+    curvs = [jnp.zeros((resp, LANES), F32)] * CORES
+    weights = [jnp.zeros((1, LANES), F32)] * CORES
+
+    def weigh_image(i, j):
+        weight, image = w[j], xfull[1, j]
         scaled = weight * image
-        sums[0] = sums[0] + scaled * image
-        sums[1] = sums[1] + weight
+        curvs[i] = curvs[i] + scaled * image
+        weights[i] = weights[i] + weight
         put_pair(j, scaled)
 
-    x_chunks(X2, 1, weigh_image)
-    curv, weight_sum = sums
+    x_halves(BACK2, 1, weigh_image)
+    curv, weight_sum = curvs[0] + curvs[1], weights[0] + weights[1]
     row_y[y] = to_row(jnp.sum(curv, axis=1, keepdims=True)) + jnp.where(
         lane[0:1] == resp, jnp.sum(weight_sum, axis=1, keepdims=True), 0.0)
     for dy in far_first(ny):
@@ -274,10 +273,10 @@
         send(SCAL_Z, row_z.at[z], row_z.at[z], at_yz(0, dz))
     z_reduce(Y2, Z2, 1)
 
-    drain(row_x.at[0, pl.ds(0, nc - 1)], recv_sem.at[GAMMA])
+    drain(row_x.at[pl.ds(0, nc - 1)], recv_sem.at[GAMMA])
     drain(row_z.at[pl.ds(0, nz - 1)], recv_sem.at[SCAL_Z])
     sums = jnp.sum(row_z[...], axis=0)
-    gamma_raw = to_column(jnp.sum(row_x[0], axis=0))
+    gamma_raw = to_column(jnp.sum(row_x[...], axis=0))
     curv_raw = to_column(sums)
     mean = jnp.sum(jnp.where(lane[0:1] == resp, sums, 0.0), axis=1, keepdims=True) / all_rows
     gamma = gamma_raw / (mean * mean)
@@ -285,34 +284,45 @@
     ratio = alpha / mean
     coef_out[...] = coef[...] + alpha * (g[...] / mean)
     for j in range(row_tiles):
-        resid_out[:, j * LANES:(j + 1) * LANES] = resid[j] - alpha * (whole[j] / mean)
-    spread_out(Z2, G2, 1)
+        resid_out[:, j * LANES:(j + 1) * LANES] = resid[j] - alpha * (xfull[1, j] / mean)
+
+    def piece_of_next(total):
+        return g[:, tile_at(y * pieces + my_piece)] - ratio * total
+
+    piece = spread_out(Z2, G2, 1, piece_of_next)
+    slot = col * ny * pieces + y * pieces + my_piece
+    row_sq[slot] = to_row(jnp.sum(piece * piece, axis=1, keepdims=True))
+
+    def send_square(dc, dy, dz):
+        send(SQUARE, row_sq.at[slot], row_sq.at[slot], (at_yz(dy, dz)[0], lax.rem(col + dc, nc)))
+
+    def to_column_block(k, _):
+        dc = nc // 2 + lax.div(k + 1, 2) * (2 * lax.rem(k, 2) - 1)
+        for dy, dz in [*spread, (0, 0)]:
+            send_square(dc, dy, dz)
+        return 0
+
+    lax.fori_loop(0, nc - 1, to_column_block, 0)
+    for dy, dz in spread:
+        send_square(0, dy, dz)
     for dy in by_arrival:
         collect(G2, 1, dy)
-
-    norm2 = jnp.zeros((resp, LANES), F32)
+    drain(row_sq.at[pl.ds(0, nc * ny * pieces - 1)], recv_sem.at[SQUARE])
+    square = to_column(jnp.sum(row_sq[...], axis=0))
+    beta = square / (mean * mean) / gamma
     for other in range(ny):
         for p in range(pieces):
             lanes = slice(other * quarter + p * LANES, other * quarter + (p + 1) * LANES)
-            piece = g[:, lanes] - ratio * gath[1, other, p]
-            gn[:, lanes] = piece
-            norm2 = norm2 + piece * piece
-    row_x[1, col] = to_row(jnp.sum(norm2, axis=1, keepdims=True))
-    for mate in col_mates:
-        send(SQUARE, row_x.at[1, col], row_x.at[1, col], mate)
-    drain(row_x.at[1, pl.ds(0, nc - 1)], recv_sem.at[SQUARE])
-    square = to_column(jnp.sum(row_x[1], axis=0))
-    beta = square / (mean * mean) / gamma
-    dir_out[...] = gn[...] / mean + beta * (g[...] / mean)
+            dir_out[:, lanes] = gath[1, other, p] / mean + beta * (g[:, lanes] / mean)
 
     for which, ref in (
-        (Y1, yrecv.at[0, pl.ds(0, ny - 1)]), (Y2, yrecv.at[1, pl.ds(0, ny - 1)]),
-        (Z1, zrecv.at[0, pl.ds(0, nz - 1)]), (Z2, zrecv.at[1, pl.ds(0, nz - 1)]),
-        (GAMMA, row_x.at[0, pl.ds(0, nc - 1)]), (SQUARE, row_x.at[1, pl.ds(0, nc - 1)]),
-        (SCAL_Y, row_y.at[pl.ds(0, ny - 1)]), (SCAL_Z, row_z.at[pl.ds(0, nz - 1)]),
-        *((base + k, crecv.at[0, pl.ds(0, step_tiles)]) for base in (CORE1, CORE2) for k in range(CHUNKS)),
-        *((base + k, xsum.at[0, pl.ds(0, nx - 1), pl.ds(0, step_tiles)]) for base in (X1, X2) for k in range(CHUNKS)),
+        *((which, crecv.at[0]) for which in (CORE1, BACK1, CORE2, BACK2)),
+        *((which, xsum.at[0, pl.ds(0, nx - 1)]) for which in (X1, X2)),
+        *((which, yrecv.at[0, pl.ds(0, ny - 1)]) for which in (Y1, Y2)),
+        *((which, zrecv.at[0, pl.ds(0, nz - 1)]) for which in (Z1, Z2)),
         *((base + k, zrecv.at[0, pl.ds(0, pieces if k else pieces - 1)]) for base in (G1, G2) for k in range(ny)),
+        (GAMMA, row_x.at[pl.ds(0, nc - 1)]), (SCAL_Y, row_y.at[pl.ds(0, ny - 1)]), (SCAL_Z, row_z.at[pl.ds(0, nz - 1)]),
+        (SQUARE, row_sq.at[pl.ds(0, nc * ny * pieces - 1)]),
     ):
         drain(ref, send_sem.at[which])
 
@@ -353,24 +363,24 @@
             vmem((resp, feats), BF16),
             vmem((resp, rows_here), F32),
             vmem((resp, feats), F32),
-            vmem((row_tiles, LANES), F32),
+            vmem((row_tiles, 1, LANES), F32),
             vmem((row_tiles, resp, LANES), F32),
             vmem((2 * resp, rows_here), BF16),
             vmem((resp, feats), F32),
-            vmem((resp, feats), F32),
             vmem((2, row_tiles, resp, LANES), F32),
-            vmem((row_tiles, resp, LANES), F32),
+            vmem((2, row_tiles // CORES, resp, LANES), F32),
+            vmem((2, nc // CORES, row_tiles // CORES, resp, LANES), F32),
             vmem((2, row_tiles, resp, LANES), F32),
-            vmem((2, nc // CORES, row_tiles, resp, LANES), F32),
             vmem((2, ny, pieces, resp, LANES), F32),
             vmem((2, ny, pieces, resp, LANES), F32),
             vmem((2, pieces, resp, LANES), F32),
             vmem((2, max(nz, ny * pieces), resp, LANES), F32),
             vmem((2, ny, pieces, resp, LANES), F32),
-            vmem((2, nc, 1, LANES), F32),
+            vmem((nc, 1, LANES), F32),
             vmem((ny, 1, LANES), F32),
             vmem((nz, 1, LANES), F32),
-            pltpu.SemaphoreType.DMA((3 + CHUNKS,)),
+            vmem((nc * ny * pieces, 1, LANES), F32),
+            pltpu.SemaphoreType.DMA((3 + CORES,)),
             pltpu.SemaphoreType.DMA((N_SEMS,)),
             pltpu.SemaphoreType.DMA((N_SEMS,)),
             pltpu.SemaphoreType.REGULAR((4,)),

time: 70.6 us -> 69.8 us (0.989)
  Pallas kernels: 69.8 us -> 69 us
    pallas_call x1, Pallas kernels: 68.1 us -> 67.2 us  [shards(): pl.pallas_call(functools.partial(kernel, ny, nz, nc, resp, float(all_rows...]
where the time goes in v4:
time: 69.8 us; the launch traced here: 69.6 us
  Pallas kernels  69 us (99%)
    pallas_call x1, Pallas kernels, shards(): pl.pallas_call(functools.partial(kernel, ny, nz, nc, resp, float(all_rows...  67.2 us
    pallas_call x1, Pallas kernels, shards(): pl.pallas_call(write_out, out_shape=outs, in_specs=[pl.BlockSpec(memory_s...  1.75 us

profile of v4, /device:TPU:1, one launch (start us, length us, event | category | flops | bytes accessed | tf_op | source)
XLA Modules:
  0.0 69.6 jit_solution(12814743507759146652)
XLA Ops:
  0.6 67.2 %shard_map.67 = (f32[16,2048]{1,0:T(8,128)}, f32[16,1024]{1,0:T(8,128)}, f32[16,2048]{1,0:T(8,128)}) custom-call(bf16[1024,2048]{1,0:T(8,128)(2,1)} %e_hbm.1, f32[16,1024]{1,0:T(8,128)} %bitcast.7, s32[8,128]{1,0:T(8,128)} %bitcast.8, f32[16,2048]{1,0:T(8,128)} %bitcast.6), custom_call_target="tpu_custom_call" | custom-call | tf_op jit(solution)/shard_map/pallas_call | solution.py:353
  67.9 1.8 %shard_map.68 = (f32[16,2048]{1,0:T(8,128)}, f32[16,1024]{1,0:T(8,128)}, f32[16,2048]{1,0:T(8,128)}) custom-call(f32[16,2048]{1,0:T(8,128)} %get-tuple-element.9.a_in, f32[16,1024]{1,0:T(8,128)} %get-tuple-element.10.b_in, f32[16,2048]{1,0:T(8,128)} %get-tuple-element.11.c_in), custom_call_target="tpu_custom_call" | custom-call | tf_op jit(solution)/shard_map/pallas_call | solution.py:391

commit v5 on v4

--- a/solution.py
+++ b/solution.py
@@ -130,12 +130,11 @@
         xfull[buf, tiles_of(core)] = total
         send(which_back, xfull.at[buf, tiles_of(core)], xfull.at[buf, tiles_of(core)], other_core)
 
-    def x_halves(which_back, buf, of_tile):
+    def x_halves(which_back, buf, of_half):
         for i, k in enumerate((core, theirs)):
             if i == 1:
                 drain(crecv.at[buf], recv_sem.at[which_back])
-            for j in range(half_tiles):
-                of_tile(i, k * half_tiles + j)
+            of_half(i, k)
             if i == 0:
                 both = jnp.dot(lhs[:, rows_of(k)], e[rows_of(k), :], preferred_element_type=F32)
                 gacc[...] = both[:resp] + both[resp:]
@@ -163,13 +162,14 @@
             send(which_z, ysum.at[buf, peer_piece], zrecv.at[buf, z], at_yz(0, dz))
         zrecv[buf, z] = ysum[buf, my_piece]
 
-    def spread_out(which_z, which_g, buf, change):
+    def spread_out(which_z, which_g, buf, change, first=lambda total: None):
         drain(zrecv.at[buf, pl.ds(0, nz - 1)], recv_sem.at[which_z])
         total = zrecv[buf, 0]
         for k in range(1, nz):
             total = total + zrecv[buf, k]
         total = change(total)
         gath[buf, y, my_piece] = total
+        first(total)
         for dy, dz in spread:
             send(which_g + dy, gath.at[buf, y, my_piece], gath.at[buf, y, my_piece], at_yz(dy, dz))
         return total
@@ -203,20 +203,21 @@
     hear(0)
     tell(1, 2 * near)
 
-    def put_pair(j, value):
-        high = value.astype(BF16)
-        low = (value - high.astype(F32)).astype(BF16)
-        lhs[0:resp, tile_at(j)] = high
-        lhs[resp:2 * resp, tile_at(j)] = low
-
-    def weigh(i, j):
-        r = t[:, tile_at(j)] - xfull[0, j]
-        resid[j] = r
-        norm = jnp.sqrt(jnp.sum(r * r, axis=0, keepdims=True))
-        weight = jnp.where(
-            cls[pl.ds(j, 1), :] == 1, huber_delta / jnp.maximum(huber_delta, norm), 1.0)
-        w[j] = weight
-        put_pair(j, weight * r)
+    def put_pairs(k, values):
+        for j, value in enumerate(values):
+            high = value.astype(BF16)
+            lhs[0:resp, tile_at(k * half_tiles + j)] = high
+            lhs[resp:2 * resp, tile_at(k * half_tiles + j)] = (value - high.astype(F32)).astype(BF16)
+
+    def weigh(i, k):
+        rs = [t[:, tile_at(k * half_tiles + j)] - xfull[0, k * half_tiles + j] for j in range(half_tiles)]
+        norm = jnp.sqrt(jnp.concatenate([jnp.sum(r * r, axis=0, keepdims=True) for r in rs], axis=0))
+        huber = jnp.where(k == 0, cls[0:half_tiles], cls[half_tiles:2 * half_tiles]) == 1
+        weight = jnp.where(huber, huber_delta / jnp.maximum(huber_delta, norm), 1.0)
+        put_pairs(k, [weight[j:j + 1] * r for j, r in enumerate(rs)])
+        w[k] = weight
+        for j, r in enumerate(rs):
+            resid[k * half_tiles + j] = r
 
     x_halves(BACK1, 0, weigh)
 
@@ -250,14 +251,16 @@
 
     x_reduce(CORE2, X2, BACK2, 1, last_product, lambda: None, send_gamma)
     curvs = [jnp.zeros((resp, LANES), F32)] * CORES
-    weights = [jnp.zeros((1, LANES), F32)] * CORES
-
-    def weigh_image(i, j):
-        weight, image = w[j], xfull[1, j]
-        scaled = weight * image
-        curvs[i] = curvs[i] + scaled * image
-        weights[i] = weights[i] + weight
-        put_pair(j, scaled)
+    weights = [None] * CORES
+
+    def weigh_image(i, k):
+        weight = w[k]
+        images = [xfull[1, k * half_tiles + j] for j in range(half_tiles)]
+        scaled = [weight[j:j + 1] * image for j, image in enumerate(images)]
+        put_pairs(k, scaled)
+        for j, image in enumerate(images):
+            curvs[i] = curvs[i] + scaled[j] * image
+        weights[i] = jnp.sum(weight, axis=0, keepdims=True)
 
     x_halves(BACK2, 1, weigh_image)
     curv, weight_sum = curvs[0] + curvs[1], weights[0] + weights[1]
@@ -289,9 +292,7 @@
     def piece_of_next(total):
         return g[:, tile_at(y * pieces + my_piece)] - ratio * total
 
-    piece = spread_out(Z2, G2, 1, piece_of_next)
     slot = col * ny * pieces + y * pieces + my_piece
-    row_sq[slot] = to_row(jnp.sum(piece * piece, axis=1, keepdims=True))
 
     def send_square(dc, dy, dz):
         send(SQUARE, row_sq.at[slot], row_sq.at[slot], (at_yz(dy, dz)[0], lax.rem(col + dc, nc)))
@@ -302,9 +303,13 @@
             send_square(dc, dy, dz)
         return 0
 
-    lax.fori_loop(0, nc - 1, to_column_block, 0)
-    for dy, dz in spread:
-        send_square(0, dy, dz)
+    def send_squares(piece):
+        row_sq[slot] = to_row(jnp.sum(piece * piece, axis=1, keepdims=True))
+        lax.fori_loop(0, nc - 1, to_column_block, 0)
+        for dy, dz in spread:
+            send_square(0, dy, dz)
+
+    spread_out(Z2, G2, 1, piece_of_next, send_squares)
     for dy in by_arrival:
         collect(G2, 1, dy)
     drain(row_sq.at[pl.ds(0, nc * ny * pieces - 1)], recv_sem.at[SQUARE])
@@ -363,7 +368,7 @@
             vmem((resp, feats), BF16),
             vmem((resp, rows_here), F32),
             vmem((resp, feats), F32),
-            vmem((row_tiles, 1, LANES), F32),
+            vmem((CORES, row_tiles // CORES, LANES), F32),
             vmem((row_tiles, resp, LANES), F32),
             vmem((2 * resp, rows_here), BF16),
             vmem((resp, feats), F32),

time: 69.8 us -> 68.9 us (0.987)
  Pallas kernels: 69 us -> 68.1 us
    pallas_call x1, Pallas kernels: 67.2 us -> 66.3 us  [shards(): pl.pallas_call(functools.partial(kernel, ny, nz, nc, resp, float(all_rows...]
where the time goes in v5:
time: 68.9 us; the launch traced here: 68.7 us
  Pallas kernels  68.1 us (99%)
    pallas_call x1, Pallas kernels, shards(): pl.pallas_call(functools.partial(kernel, ny, nz, nc, resp, float(all_rows...  66.3 us
    pallas_call x1, Pallas kernels, shards(): pl.pallas_call(write_out, out_shape=outs, in_specs=[pl.BlockSpec(memory_s...  1.75 us

profile of v5, /device:TPU:1, one launch (start us, length us, event | category | flops | bytes accessed | tf_op | source)
XLA Modules:
  0.0 68.7 jit_solution(76689428881308888)
XLA Ops:
  0.6 66.3 %shard_map.67 = (f32[16,2048]{1,0:T(8,128)}, f32[16,1024]{1,0:T(8,128)}, f32[16,2048]{1,0:T(8,128)}) custom-call(bf16[1024,2048]{1,0:T(8,128)(2,1)} %e_hbm.1, f32[16,1024]{1,0:T(8,128)} %bitcast.7, s32[8,128]{1,0:T(8,128)} %bitcast.8, f32[16,2048]{1,0:T(8,128)} %bitcast.6), custom_call_target="tpu_custom_call" | custom-call | tf_op jit(solution)/shard_map/pallas_call | solution.py:358
  67.0 1.8 %shard_map.68 = (f32[16,2048]{1,0:T(8,128)}, f32[16,1024]{1,0:T(8,128)}, f32[16,2048]{1,0:T(8,128)}) custom-call(f32[16,2048]{1,0:T(8,128)} %get-tuple-element.9.a_in, f32[16,1024]{1,0:T(8,128)} %get-tuple-element.10.b_in, f32[16,2048]{1,0:T(8,128)} %get-tuple-element.11.c_in), custom_call_target="tpu_custom_call" | custom-call | tf_op jit(solution)/shard_map/pallas_call | solution.py:396

commit v6 on v5

--- a/solution.py
+++ b/solution.py
@@ -26,11 +26,12 @@
 
 def kernel(ny, nz, nc, resp, all_rows,
            e_hbm, t_hbm, cls_hbm, c_hbm,
+           coef_hbm, resid_hbm, dir_hbm,
            coef_out, resid_out, dir_out,
            e, t, cls, coef, cb, acc, gacc, w, resid, lhs, g,
            part, crecv, xsum, xfull, yrecv, ypart, ysum, zrecv, gath,
            row_x, row_y, row_z, row_sq,
-           load_sem, send_sem, recv_sem, near_sem):
+           load_sem, send_sem, recv_sem, near_sem, out_sem):
     rows_here, feats = e.shape
     row_tiles = rows_here // LANES
     half_rows = rows_here // CORES
@@ -288,6 +289,10 @@
     coef_out[...] = coef[...] + alpha * (g[...] / mean)
     for j in range(row_tiles):
         resid_out[:, j * LANES:(j + 1) * LANES] = resid[j] - alpha * (xfull[1, j] / mean)
+    stores = [pltpu.make_async_copy(src, dst, out_sem.at[k]) for k, (src, dst) in enumerate(
+        ((coef_out, coef_hbm), (resid_out, resid_hbm), (dir_out, dir_hbm)))]
+    stores[0].start()
+    stores[1].start()
 
     def piece_of_next(total):
         return g[:, tile_at(y * pieces + my_piece)] - ratio * total
@@ -319,6 +324,7 @@
         for p in range(pieces):
             lanes = slice(other * quarter + p * LANES, other * quarter + (p + 1) * LANES)
             dir_out[:, lanes] = gath[1, other, p] / mean + beta * (g[:, lanes] / mean)
+    stores[2].start()
 
     for which, ref in (
         *((which, crecv.at[0]) for which in (CORE1, BACK1, CORE2, BACK2)),
@@ -330,15 +336,21 @@
         (SQUARE, row_sq.at[pl.ds(0, nc * ny * pieces - 1)]),
     ):
         drain(ref, send_sem.at[which])
-
-
-def write_out(a_in, b_in, c_in, a_out, b_out, c_out, sems):
-    copies = [pltpu.make_async_copy(src, dst, sems.at[k])
-              for k, (src, dst) in enumerate(((a_in, a_out), (b_in, b_out), (c_in, c_out)))]
-    for copy in copies:
-        copy.start()
-    for copy in copies:
-        copy.wait()
+    for store in stores:
+        store.wait()
+
+
+def write_out(a_in, b_in, c_in, a_out, b_out, c_out, a, b, c, sems):
+    moves = ((a_in, a, a_out), (b_in, b, b_out), (c_in, c, c_out))
+    loads = [pltpu.make_async_copy(src, held, sems.at[0, k]) for k, (src, held, _) in enumerate(moves)]
+    stores = [pltpu.make_async_copy(held, dst, sems.at[1, k]) for k, (_, held, dst) in enumerate(moves)]
+    for load in loads:
+        load.start()
+    for load, store in zip(loads, stores):
+        load.wait()
+        store.start()
+    for store in stores:
+        store.wait()
 
 
 def shards(ny, embeddings, targets, classes, start_coef):
@@ -359,8 +371,9 @@
         functools.partial(kernel, ny, nz, nc, resp, float(all_rows)),
         out_shape=outs,
         in_specs=[pl.BlockSpec(memory_space=pltpu.HBM)] * 4,
-        out_specs=(pl.BlockSpec(memory_space=pltpu.VMEM),) * 3,
+        out_specs=(pl.BlockSpec(memory_space=pl.ANY),) * 3,
         scratch_shapes=[
+            *(vmem(out.shape, F32) for out in outs),
             vmem((rows_here, feats), BF16),
             vmem((resp, rows_here), F32),
             vmem((row_tiles, LANES), jnp.int32),
@@ -389,6 +402,7 @@
             pltpu.SemaphoreType.DMA((N_SEMS,)),
             pltpu.SemaphoreType.DMA((N_SEMS,)),
             pltpu.SemaphoreType.REGULAR((4,)),
+            pltpu.SemaphoreType.DMA((3,)),
         ],
         compiler_params=pltpu.CompilerParams(
             collective_id=0, has_side_effects=True, vmem_limit_bytes=60 * 1024 * 1024),
@@ -396,9 +410,9 @@
     results = pl.pallas_call(
         write_out,
         out_shape=outs,
-        in_specs=[pl.BlockSpec(memory_space=pltpu.VMEM)] * 3,
+        in_specs=[pl.BlockSpec(memory_space=pl.ANY)] * 3,
         out_specs=(pl.BlockSpec(memory_space=pl.ANY),) * 3,
-        scratch_shapes=[pltpu.SemaphoreType.DMA((3,))],
+        scratch_shapes=[*(vmem(out.shape, F32) for out in outs), pltpu.SemaphoreType.DMA((2, 3))],
         compiler_params=pltpu.CompilerParams(vmem_limit_bytes=60 * 1024 * 1024),
     )(*results)
     return tuple(out.T for out in results)

time: 68.9 us -> 68.8 us (level)
  no operation moved by 1% of the time
where the time goes in v6:
time: 68.8 us; the launch traced here: 68.6 us
  Pallas kernels  68 us (99%)
    pallas_call x1, Pallas kernels, shards(): pl.pallas_call(functools.partial(kernel, ny, nz, nc, resp, float(all_rows...  66.3 us
    pallas_call x1, Pallas kernels, shards(): pl.pallas_call(write_out, out_shape=outs, in_specs=[pl.BlockSpec(memory_s...  1.71 us

profile of v6, /device:TPU:1, one launch (start us, length us, event | category | flops | bytes accessed | tf_op | source)
XLA Modules:
  0.0 68.6 jit_solution(774837161922280646)
XLA Ops:
  0.6 66.3 %shard_map.67 = (f32[16,2048]{1,0:T(8,128)}, f32[16,1024]{1,0:T(8,128)}, f32[16,2048]{1,0:T(8,128)}) custom-call(bf16[1024,2048]{1,0:T(8,128)(2,1)} %e_hbm.1, f32[16,1024]{1,0:T(8,128)} %bitcast.7, s32[8,128]{1,0:T(8,128)} %bitcast.8, f32[16,2048]{1,0:T(8,128)} %bitcast.6), custom_call_target="tpu_custom_call" | custom-call | tf_op jit(solution)/shard_map/pallas_call | solution.py:370
  66.9 1.7 %shard_map.68 = (f32[16,2048]{1,0:T(8,128)}, f32[16,1024]{1,0:T(8,128)}, f32[16,2048]{1,0:T(8,128)}) custom-call(f32[16,2048]{1,0:T(8,128)} %get-tuple-element.9.a_in, f32[16,1024]{1,0:T(8,128)} %get-tuple-element.10.b_in, f32[16,2048]{1,0:T(8,128)} %get-tuple-element.11.c_in), custom_call_target="tpu_custom_call" | custom-call | tf_op jit(solution)/shard_map/pallas_call | solution.py:410

commit v7 on v6

--- a/solution.py
+++ b/solution.py
@@ -317,13 +317,15 @@
     spread_out(Z2, G2, 1, piece_of_next, send_squares)
     for dy in by_arrival:
         collect(G2, 1, dy)
+    for other in range(ny):
+        for p in range(pieces):
+            lanes = slice(other * quarter + p * LANES, other * quarter + (p + 1) * LANES)
+            dir_out[:, lanes] = gath[1, other, p] / mean
+            g[:, lanes] = g[:, lanes] / mean
     drain(row_sq.at[pl.ds(0, nc * ny * pieces - 1)], recv_sem.at[SQUARE])
     square = to_column(jnp.sum(row_sq[...], axis=0))
     beta = square / (mean * mean) / gamma
-    for other in range(ny):
-        for p in range(pieces):
-            lanes = slice(other * quarter + p * LANES, other * quarter + (p + 1) * LANES)
-            dir_out[:, lanes] = gath[1, other, p] / mean + beta * (g[:, lanes] / mean)
+    dir_out[...] = dir_out[...] + beta * g[...]
     stores[2].start()
 
     for which, ref in (

time: 68.8 us -> 68.8 us (level)
  no operation moved by 1% of the time
where the time goes in v7:
time: 68.8 us; the launch traced here: 68.6 us
  Pallas kernels  68 us (99%)
    pallas_call x1, Pallas kernels, shards(): pl.pallas_call(functools.partial(kernel, ny, nz, nc, resp, float(all_rows...  66.3 us
    pallas_call x1, Pallas kernels, shards(): pl.pallas_call(write_out, out_shape=outs, in_specs=[pl.BlockSpec(memory_s...  1.71 us

profile of v7, /device:TPU:1, one launch (start us, length us, event | category | flops | bytes accessed | tf_op | source)
XLA Modules:
  0.0 68.6 jit_solution(4487489675498711106)
XLA Ops:
  0.6 66.3 %shard_map.67 = (f32[16,2048]{1,0:T(8,128)}, f32[16,1024]{1,0:T(8,128)}, f32[16,2048]{1,0:T(8,128)}) custom-call(bf16[1024,2048]{1,0:T(8,128)(2,1)} %e_hbm.1, f32[16,1024]{1,0:T(8,128)} %bitcast.7, s32[8,128]{1,0:T(8,128)} %bitcast.8, f32[16,2048]{1,0:T(8,128)} %bitcast.6), custom_call_target="tpu_custom_call" | custom-call | tf_op jit(solution)/shard_map/pallas_call | solution.py:372
  66.9 1.7 %shard_map.68 = (f32[16,2048]{1,0:T(8,128)}, f32[16,1024]{1,0:T(8,128)}, f32[16,2048]{1,0:T(8,128)}) custom-call(f32[16,2048]{1,0:T(8,128)} %get-tuple-element.9.a_in, f32[16,1024]{1,0:T(8,128)} %get-tuple-element.10.b_in, f32[16,2048]{1,0:T(8,128)} %get-tuple-element.11.c_in), custom_call_target="tpu_custom_call" | custom-call | tf_op jit(solution)/shard_map/pallas_call | solution.py:412
